TPU v7x, 128 devices: a whole 4x4x4 slice. The times are simulated.
128 devices in a mesh: aux: 8 (over y, x_lo), row: 8 (over z, core), col: 2 (over x_hi).
Axes of the slice: x: 4 (x_hi: 2, x_lo: 2; x = x_hi * 2 + x_lo), y: 4, z: 4, core: 2. Of those that a mesh axis runs over, the one named last changes fastest.
Arguments:
- b_tensor: bfloat16 [16, 6144, 1024], P('aux', 'row', 'col'), may hold values from -0.046875 to 0.046875
- hcore: float32 [6144, 6144], P('row', ('aux', 'col')), may hold values from -0.078125 to 0.078125
- c_occ: float32 [6144, 1024], P('row'), may hold values from -6 to 6
- c_virt: float32 [6144, 5120], P(('aux', 'col')), may hold values from -6 to 6
- eps_occ: float32 [1024], P('row'), may hold values from -3 to -0.5
- eps_virt: float32 [5120], P(('aux', 'col')), may hold values from 0.5 to 3
Outputs:
- c_new: float32 [6144, 1024], P(('aux', 'col'), 'row')
All inputs are finite; a program needn't handle non-finite values.
Results may differ from a plain program's by a relative error of at most 0.0003.
Values may be sent and summed in bfloat16 or wider, within the bound.
A program may use at most 128 MiB of HBM per device.

v0:
```python
import jax
import jax.numpy as jnp
from jax import lax
from jax.sharding import PartitionSpec as P

O = 1024
TAYLOR = 8
V = 5120


rotation_scale = 0.03


def spread(value, axis, source):
    kept = jnp.where(lax.axis_index(axis) == source, value, 0).astype(value.dtype)
    return lax.psum(kept, axis)


def occ_partial(kappa_rows, virt_term, order):
    local_term = -jnp.einsum(
        "ai,aj->ij", kappa_rows, virt_term, precision=lax.Precision.HIGHEST
    ) / float(order)
    return lax.psum(local_term, ("aux", "col"))


def on_device(b_tensor, hcore, c_occ, c_virt, eps_occ, eps_virt):
    high = lax.Precision.HIGHEST
    terms = jnp.einsum(
        "pmi,pni->mn",
        b_tensor,
        lax.all_gather(b_tensor, "row", axis=1, tiled=True),
        preferred_element_type=jnp.float32,
    )
    exchange = lax.psum_scatter(terms, ("aux", "col"), scatter_dimension=1, tiled=True)
    fock = hcore - exchange
    row_count = c_occ.shape[0]
    col_count = fock.shape[1]
    block_index = lax.axis_index(("aux", "col"))
    first_row = block_index * col_count
    owner = first_row // row_count
    own_slice = lax.dynamic_slice_in_dim(c_occ, first_row % row_count, col_count, 0)
    occ_cols = spread(own_slice, "row", owner)
    occ_image = lax.psum_scatter(
        jnp.dot(fock.T, c_occ, precision=high), "row", scatter_dimension=1, tiled=True
    )
    gradient = lax.psum_scatter(
        jnp.dot(c_virt.T, occ_image, precision=high),
        ("aux", "col"),
        scatter_dimension=0,
        tiled=True,
    )
    scaled = gradient / (eps_virt[:, None] - eps_occ[None, :])
    meansq = lax.psum(jnp.sum(scaled * scaled), ("aux", "row", "col")) / (V * O)
    kappa = rotation_scale * scaled / jnp.sqrt(meansq + 1e-06)
    kappa_rows = lax.all_gather(kappa, "row", axis=1, tiled=True)
    occ_width = kappa.shape[1]
    offset = lax.axis_index("row") * occ_width
    occ_sum = (
        jnp.arange(O, dtype=jnp.int32)[:, None]
        == (offset + jnp.arange(occ_width, dtype=jnp.int32))[None, :]
    ).astype(jnp.float32)
    virt_term = kappa
    virt_sum = kappa
    occ_term = occ_sum
    for order in range(2, TAYLOR + 1):
        if order % 2 == 0:
            occ_term = occ_partial(kappa_rows, virt_term, order)
            occ_sum = occ_sum + occ_term
        else:
            virt_term = jnp.dot(kappa_rows, occ_term, precision=high) / float(order)
            virt_sum = virt_sum + virt_term
    initial = jnp.dot(occ_cols, occ_sum, precision=high)
    return initial + jnp.dot(
        c_virt, lax.all_gather(virt_sum, ("aux", "col"), axis=0, tiled=True), precision=high
    )


def solution(mesh):
    placed = (
        P("aux", "row", "col"),
        P("row", ("aux", "col")),
        P("row", None),
        P(("aux", "col"), None),
        P("row"),
        P(("aux", "col")),
    )
    return jax.shard_map(
        on_device, mesh=mesh, in_specs=placed, out_specs=P(("aux", "col"), "row"), check_vma=False
    )
```

profile of v0, /device:TPU:1, one launch (start us, length us, event | category | flops | bytes accessed | tf_op | source)
XLA Modules:
  0.0 1238.9 jit_solution(4701202955505461506)
XLA Ops:
  7.3 72.9 %all-gather.4.cloned.1.call-done = bf16[2,6144,512]{2,1,0:T(8,128)(2,1)} async-done(((bf16[2,768,512]{2,1,0:T(8,128)(2,1)}), bf16[2,6144,512]{2,1,0:T(8,128)(2,1)}) %all-gather.4.cloned.1.call-update) | async-done | bytes 12582928 | tf_op jit(solution)/shard_map/all_gather | solution.py:31
  80.2 16.5 %convolution_bitcast_fusion = f32[768,6144]{1,0:T(8,128)} fusion(bf16[2,768,512]{2,1,0:T(8,128)(2,1)S(1)} %copy-done.6, bf16[2,6144,512]{2,1,0:T(8,128)(2,1)} %all-gather.4.cloned.1.call-done), kind=kOutput, calls=%fused_computation | convolution fusion | flops 9663676416 | bytes 33030144 | tf_op jit(solution)/shard_map/pmi,pni->mn/dot_general | solution.py:28
  96.8 394.5 %reduce-scatter.6.cloned.1.call-done = f32[768,384]{1,0:T(8,128)} async-done(((f32[768,6144]{1,0:T(8,128)}), f32[768,384]{1,0:T(8,128)}) %reduce-scatter.6.cloned.1.call-update) | async-done | bytes 1179664 | tf_op jit(solution)/shard_map/reduce_scatter | solution.py:34
  491.3 6.7 fusion.4
  498.1 27.2 %reduce-scatter.8.cloned.1.call-done = f32[384,128]{1,0:T(8,128)} async-done(((f32[384,1024]{1,0:T(8,128)}), f32[384,128]{1,0:T(8,128)}) %reduce-scatter.8.cloned.1.call-update) | async-done | bytes 196624 | tf_op jit(solution)/shard_map/reduce_scatter | solution.py:43
  525.4 7.1 convolution_bitcast_fusion.1
  534.7 85.7 %reduce-scatter.10.cloned.1.call-done = f32[320,128]{1,0:T(8,128)} async-done(((f32[5120,128]{1,0:T(8,128)}), f32[320,128]{1,0:T(8,128)}) %reduce-scatter.10.cloned.1.call-update) | async-done | bytes 163856 | tf_op jit(solution)/shard_map/reduce_scatter | solution.py:46
  622.0 70.2 %psum.43 = f32[]{:T(128)} all-reduce(f32[]{:T(128)} %multiply_reduce_fusion), channel_id=1, replica_groups=mesh['aux'=8,'row'=8,'col'=2] {'aux','row','col'}, use_global_device_ids=true, to_apply=%region_5.6 | all-reduce | flops 1 | bytes 8 | tf_op jit(solution)/shard_map/psum | solution.py:53
  694.9 22.1 %all-gather.6.cloned.1.call-done = f32[320,1024]{1,0:T(8,128)} async-done(((f32[320,128]{1,0:T(8,128)}), f32[320,1024]{1,0:T(8,128)}) %all-gather.6.cloned.1.call-update) | async-done | bytes 1310736 | tf_op jit(solution)/shard_map/all_gather | solution.py:55
  717.1 4.9 fusion.3
  722.0 84.2 %all-reduce.8.cloned.1.call-done = f32[1024,128]{1,0:T(8,128)} async-done(((f32[1024,128]{1,0:T(8,128)}), f32[1024,128]{1,0:T(8,128)}) %all-reduce.8.cloned.1.call-update) | async-done | bytes 524304 | tf_op jit(solution)/shard_map/psum | solution.py:23
  806.2 2.2 convolution_multiply_fusion.2
  808.5 3.4 fusion.2
  812.0 84.5 %all-reduce.10.cloned.1.call-done = f32[1024,128]{1,0:T(8,128)} async-done(((f32[1024,128]{1,0:T(8,128)}), f32[1024,128]{1,0:T(8,128)}) %all-reduce.10.cloned.1.call-update) | async-done | bytes 524304 | tf_op jit(solution)/shard_map/psum | solution.py:23
  898.7 3.4 fusion.1
  902.3 2.9 dynamic-slice_select_fusion
  905.5 81.2 %all-reduce.12.cloned.1.call-done = f32[1024,128]{1,0:T(8,128)} async-done(((f32[1024,128]{1,0:T(8,128)}), f32[1024,128]{1,0:T(8,128)}) %all-reduce.12.cloned.1.call-update) | async-done | bytes 524304 | tf_op jit(solution)/shard_map/psum | solution.py:23
  986.7 2.9 add_add_fusion
  989.6 3.5 fusion
  993.8 58.4 %all-reduce.6.cloned.1.call-done = f32[384,1024]{1,0:T(8,128)} async-done(((f32[384,1024]{1,0:T(8,128)}), f32[384,1024]{1,0:T(8,128)}) %all-reduce.6.cloned.1.call-update) | async-done | bytes 1572880 | tf_op jit(solution)/shard_map/psum | solution.py:16
  1052.3 88.3 %all-reduce.14.cloned.1.call-done = f32[1024,128]{1,0:T(8,128)} async-done(((f32[1024,128]{1,0:T(8,128)}), f32[1024,128]{1,0:T(8,128)}) %all-reduce.14.cloned.1.call-update) | async-done | bytes 524304 | tf_op jit(solution)/shard_map/psum | solution.py:23
  1140.6 2.9 fusion.7
  1143.5 79.0 %all-gather.8.cloned.1.call-done = f32[5120,128]{1,0:T(8,128)} async-done(((f32[320,128]{1,0:T(8,128)}), f32[5120,128]{1,0:T(8,128)}) %all-gather.8.cloned.1.call-update) | async-done | bytes 2621456 | tf_op jit(solution)/shard_map/all_gather | solution.py:74
  1222.6 9.8 fusion.6
  (45 shorter events, 10.1 us)
Async XLA Ops:
  6.5 73.7 %copy-start.6 = (bf16[2,768,512]{2,1,0:T(8,128)(2,1)S(1)}, bf16[2,768,512]{2,1,0:T(8,128)(2,1)}, u32[]{:S(2)}) copy-start(bf16[2,768,512]{2,1,0:T(8,128)(2,1)} %param.6) | copy-start | bytes 4718596
  6.5 73.7 %all-gather.4.cloned.1.call-start = ((), (), s32[]{:S(2)}) async-start(), calls=%async_computation.4 | async-start | bytes 14155776 | tf_op jit(solution)/shard_map/all_gather | solution.py:31
  7.3 484.1 %reduce-scatter.6.cloned.1.call-start = ((), (), s32[]{:S(2)}) async-start(), calls=%async_computation.5 | async-start | bytes 20054016 | tf_op jit(solution)/shard_map/reduce_scatter | solution.py:34
  96.7 394.6 %copy-start.1 = (f32[768,1024]{1,0:T(8,128)S(1)}, f32[768,1024]{1,0:T(8,128)}, u32[]{:S(2)}) copy-start(f32[768,1024]{1,0:T(8,128)} %param.8) | copy-start | bytes 9437188
  96.7 428.6 %reduce-scatter.8.cloned.1.call-start = ((), (), s32[]{:S(2)}) async-start(), calls=%async_computation.6 | async-start | bytes 1769472 | tf_op jit(solution)/shard_map/reduce_scatter | solution.py:43
  498.1 122.3 %reduce-scatter.10.cloned.1.call-start = ((), (), s32[]{:S(2)}) async-start(), calls=%async_computation.13 | async-start | bytes 2785280 | tf_op jit(solution)/shard_map/reduce_scatter | solution.py:46
  534.6 85.8 %copy-start.7 = (f32[320]{0:T(512)S(1)}, f32[320]{0:T(512)}, u32[]{:S(2)}) copy-start(f32[320]{0:T(512)} %param.11) | copy-start | bytes 3844
  534.6 85.8 %copy-start.8 = (f32[128]{0:T(128)S(1)}, f32[128]{0:T(128)}, u32[]{:S(2)}) copy-start(f32[128]{0:T(128)} %param.10) | copy-start | bytes 1540
  534.6 182.4 %all-gather.6.cloned.1.call-start = ((), (), s32[]{:S(2)}) async-start(), calls=%async_computation.7 | async-start | bytes 1474560 | tf_op jit(solution)/shard_map/all_gather | solution.py:55
  694.7 111.5 %all-reduce.8.cloned.1.call-start = ((), (), s32[]{:S(2)}) async-start(), calls=%async_computation.8 | async-start | bytes 1048576 | tf_op jit(solution)/shard_map/psum | solution.py:23
  717.1 89.2 %copy-start = (f32[320,1024]{1,0:T(8,128)S(1)}, f32[320,1024]{1,0:T(8,128)}, u32[]{:S(2)}) copy-start(f32[320,1024]{1,0:T(8,128)} %all-gather.6.cloned.1.call-done) | copy-start | bytes 3932164
  722.0 174.5 %all-reduce.10.cloned.1.call-start = ((), (), s32[]{:S(2)}) async-start(), calls=%async_computation.9 | async-start | bytes 1048576 | tf_op jit(solution)/shard_map/psum | solution.py:23
  812.0 174.7 %all-reduce.12.cloned.1.call-start = ((), (), s32[]{:S(2)}) async-start(), calls=%async_computation.10 | async-start | bytes 1048576 | tf_op jit(solution)/shard_map/psum | solution.py:23
  902.2 150.1 %all-reduce.6.cloned.1.call-start = ((), (), s32[]{:S(2)}) async-start(), calls=%async_computation.3 | async-start | bytes 3145728 | tf_op jit(solution)/shard_map/psum | solution.py:16
  905.2 81.5 %copy-start.2 = (f32[320,128]{1,0:T(8,128)S(1)}, f32[320,128]{1,0:T(8,128)}, u32[]{:S(2)}) copy-start(f32[320,128]{1,0:T(8,128)} %multiply_divide_fusion) | copy-start | bytes 491524
  905.2 235.4 %all-reduce.14.cloned.1.call-start = ((), (), s32[]{:S(2)}) async-start(), calls=%async_computation.11 | async-start | bytes 1048576 | tf_op jit(solution)/shard_map/psum | solution.py:23
  989.6 151.0 %copy-start.3 = (f32[1024,128]{1,0:T(8,128)S(1)}, f32[1024,128]{1,0:T(8,128)}, u32[]{:S(2)}) copy-start(f32[1024,128]{1,0:T(8,128)} %all-reduce.8.cloned.1.call-done) | copy-start | bytes 1572868
  989.6 151.0 %copy-start.4 = (f32[1024,128]{1,0:T(8,128)S(1)}, f32[1024,128]{1,0:T(8,128)}, u32[]{:S(2)}) copy-start(f32[1024,128]{1,0:T(8,128)} %all-reduce.10.cloned.1.call-done) | copy-start | bytes 1572868
  989.6 151.0 %copy-start.5 = (f32[1024,128]{1,0:T(8,128)S(1)}, f32[1024,128]{1,0:T(8,128)}, u32[]{:S(2)}) copy-start(f32[1024,128]{1,0:T(8,128)} %all-reduce.12.cloned.1.call-done) | copy-start | bytes 1572868
  993.1 229.5 %all-gather.8.cloned.1.call-start = ((), (), s32[]{:S(2)}) async-start(), calls=%async_computation.12 | async-start | bytes 2785280 | tf_op jit(solution)/shard_map/all_gather | solution.py:74
Sparse Core Ops, SparseCore 0:
  9.0 71.1 all-gather.3
  96.9 394.4 reduce-scatter.5
  498.2 27.1 reduce-scatter.7
  534.7 85.5 reduce-scatter.9
  694.8 22.2 all-gather.5
  722.1 84.0 all-reduce.7
  812.1 84.3 all-reduce.9
  902.3 84.3 all-reduce.11
  989.2 63.0 all-reduce.5
  1055.7 84.8 all-reduce.13
  1142.2 80.2 all-gather.7
where the time goes:
time: 1250 us; the launch traced here: 1240 us
  waiting for transfers between devices  1080 us (86%)
  blocking collectives  70.2 us (6%)
  matrix products  65.7 us (5%)
  between operations  14 us (1%)
    reduce_scatter x1, waiting for transfers between devices, on_device(): lax.psum_scatter(terms, ('aux', 'col'), scatter_dimension=1, tiled=True)  395 us
    psum x4, waiting for transfers between devices, occ_partial(): return lax.psum(local_term, ('aux', 'col'))  338 us
    reduce_scatter x1, waiting for transfers between devices, on_device(): lax.psum_scatter(jnp.dot(c_virt.T, occ_image, precision=high), ('aux', 'c...  85.7 us
    all_gather x1, waiting for transfers between devices, on_device(): lax.all_gather(virt_sum, ('aux', 'col'), axis=0, tiled=True)  79 us
    all_gather x1, waiting for transfers between devices, on_device(): lax.all_gather(b_tensor, 'row', axis=1, tiled=True)  72.9 us
    psum x1, blocking collectives, on_device(): meansq = lax.psum(jnp.sum(scaled * scaled), ('aux', 'row', 'col')) / (V * O)  70.2 us
    psum x1, waiting for transfers between devices, spread(): return lax.psum(kept, axis)  58.4 us
    reduce_scatter x1, waiting for transfers between devices, on_device(): lax.psum_scatter(jnp.dot(fock.T, c_occ, precision=high), 'row', scatter_d...  27.2 us
  transfers between devices with their start and end apart: 11, of which 11 were waited for; matrix products, arithmetic and copies ran while one was open for 1% of the time, Pallas kernels for 0%

commit v1 on v0

v1 whole, which is shorter than its diff:
```python
import functools

import jax
import jax.numpy as jnp
from jax import lax
from jax.experimental import pallas as pl
from jax.experimental.pallas import tpu as pltpu
from jax.sharding import PartitionSpec as P

ROTATION_SCALE = 0.03
MESH = pl.DeviceIdType.MESH
F32 = jnp.float32
BF16 = jnp.bfloat16
XY = ("xa", "xb", "ya", "yb")
ROW = ("za", "zb", "cc")
VMEM_LIMIT = 60 * 1024 * 1024


class Place:
    def __init__(self):
        aux, row, col = (lax.axis_index(n) for n in ("aux", "row", "col"))
        y, xl = aux // 2, aux % 2
        z, core = row // 2, row % 2
        self.aux, self.row, self.col = aux, row, col
        self.bit = {
            "xa": (xl + col) % 2, "xb": col,
            "ya": (y + y // 2) % 2, "yb": y // 2,
            "za": (z + z // 2) % 2, "zb": z // 2,
            "cc": core,
        }
        self.partner = {
            "xa": (aux + 1 - 2 * xl, row, col),
            "xb": (aux + 1 - 2 * xl, row, 1 - col),
            "ya": (aux + 2 - 4 * (y % 2), row, col),
            "yb": (2 * (3 - y) + xl, row, col),
            "za": (aux, row + 2 - 4 * (z % 2), col),
            "zb": (aux, 2 * (3 - z) + core, col),
            "cc": (aux, row + 1 - 2 * core, col),
        }

    def greet(self, dims, swap=False):
        barrier = pltpu.get_barrier_semaphore()
        for d in dims:
            pl.semaphore_signal(barrier, inc=1, device_id=self.partner[d], device_id_type=MESH)
        if not swap:
            pl.semaphore_wait(barrier, len(dims))
            return

        @pl.when(self.aux != self.row)
        def _():
            pl.semaphore_signal(
                barrier, inc=1, device_id=(self.row, self.aux, self.col), device_id_type=MESH
            )
            pl.semaphore_wait(barrier, len(dims) + 1)

        @pl.when(self.aux == self.row)
        def _():
            pl.semaphore_wait(barrier, len(dims))


def xy_bits(aux, col):
    y, xl = aux // 2, aux % 2
    return ((xl + col) % 2, col, (y + y // 2) % 2, y // 2)


def row_bits(row):
    z, core = row // 2, row % 2
    return ((z + z // 2) % 2, z // 2, core)


class Sems:
    def __init__(self, send, recv):
        self.send, self.recv, self.n = send, recv, 0

    def take(self):
        n = self.n
        self.n += 1
        return self.send.at[n], self.recv.at[n]


def scatter_stream(place, work, axes, order, tail, recvs, sems):
    done = []
    for step, d in enumerate(order):
        def index(bit_of_d):
            return tuple(
                place.bit[a] if a in done else (bit_of_d if a == d else slice(None)) for a in axes
            ) + tail
        mine, theirs = index(place.bit[d]), index(1 - place.bit[d])
        s, r = sems.take()
        copy = pltpu.make_async_remote_copy(
            src_ref=work.at[theirs], dst_ref=recvs[step], send_sem=s, recv_sem=r,
            device_id=place.partner[d], device_id_type=MESH,
        )
        copy.start()
        yield
        copy.wait()
        work[mine] = work[mine] + recvs[step][...]
        done.append(d)


def gather_stream(place, full, axes, order, tail, sems):
    done = []
    for d in order:
        sl = tuple(slice(None) if a in done else place.bit[a] for a in axes) + tail
        s, r = sems.take()
        copy = pltpu.make_async_remote_copy(
            src_ref=full.at[sl], dst_ref=full.at[sl], send_sem=s, recv_sem=r,
            device_id=place.partner[d], device_id_type=MESH,
        )
        copy.start()
        yield
        copy.wait()
        done.append(d)


def drive(streams):
    streams = list(streams)
    while streams:
        alive = []
        for g in streams:
            try:
                next(g)
                alive.append(g)
            except StopIteration:
                pass
        streams = alive


def rotate(dims, k):
    return tuple(dims[k:]) + tuple(dims[:k])


XY_ORDERS = [("xa", "ya", "xb", "yb"), ("xb", "yb", "xa", "ya"),
             ("ya", "xa", "yb", "xb"), ("yb", "xb", "ya", "xa")]
ROW_ORDERS = [("cc", "za", "zb"), ("cc", "zb", "za")]


def recv_shapes(n, block):
    return [pltpu.VMEM((2,) * (n - 1 - t) + block, F32) for t in range(n)]


def dma(n):
    return pltpu.SemaphoreType.DMA((n,))


ANY = pl.BlockSpec(memory_space=pl.ANY)
VM = pl.BlockSpec(memory_space=pltpu.VMEM)


def call(kernel, outs, in_specs, scratch, cid, *args):
    return pl.pallas_call(
        kernel,
        out_shape=outs,
        in_specs=in_specs,
        out_specs=jax.tree.map(lambda _: VM, outs),
        scratch_shapes=scratch,
        compiler_params=pltpu.CompilerParams(
            collective_id=cid, has_side_effects=True, vmem_limit_bytes=VMEM_LIMIT
        ),
    )(*args)


def split(x):
    hi = x.astype(BF16)
    return hi, (x - hi.astype(F32)).astype(BF16)


def x_kernel(x_in, hi_ref, lo_ref, work, full, r0, r1, local, send, recv):
    place = Place()
    sems = Sems(send, recv)
    load = pltpu.make_async_copy(x_in, work, local)
    load.start()
    place.greet(ROW)
    load.wait()
    rec = [r0, r1]
    axes = ROW
    drive(
        scatter_stream(place, work, axes, ROW_ORDERS[s], (pl.ds(64 * s, 64),),
                       rec[s], sems)
        for s in range(2)
    )
    mine = tuple(place.bit[d] for d in axes)
    full[mine] = work[mine]
    drive(
        gather_stream(place, full, axes, ROW_ORDERS[s][::-1], (pl.ds(64 * s, 64),), sems)
        for s in range(2)
    )
    for i in range(8):
        bits = (i // 4, (i // 2) % 2, i % 2)
        hi, lo = split(full[bits])
        hi_ref[pl.ds(128 * i, 128)] = hi
        lo_ref[pl.ds(128 * i, 128)] = lo


def x_all_reduce(x):
    n = x.shape[0]
    outs = (jax.ShapeDtypeStruct((n, n), BF16),) * 2
    rec = recv_shapes(3, (64, n))
    return call(
        lambda x_in, hi, lo, work, full, a0, a1, a2, b0, b1, b2, local, send, recv: x_kernel(
            x_in, hi, lo, work, full, [a0, a1, a2], [b0, b1, b2], local, send, recv),
        outs, [ANY],
        [pltpu.VMEM((2, 2, 2, 128, n), F32)] * 2 + rec + rec
        + [pltpu.SemaphoreType.DMA, dma(12), dma(12)],
        0, x.reshape(2, 2, 2, 128, n),
    )


def image_kernel(y_in, h_in, out, yw, hw, ybuf, *rest):
    yrec = [rest[4 * s: 4 * s + 4] for s in range(4)]
    hrec = [rest[16 + 3 * s: 19 + 3 * s] for s in range(2)]
    ylocal, hlocal, send, recv = rest[22:]
    place = Place()
    sems = Sems(send, recv)
    loads = []
    for aux in range(8):
        for half in range(2):
            loads.append(pltpu.make_async_copy(
                y_in.at[pl.ds(384 * half, 384), pl.ds(128 * aux, 128)],
                yw.at[xy_bits(aux, half)], ylocal.at[2 * aux + half]))
    for row in range(8):
        loads.append(pltpu.make_async_copy(
            h_in.at[:, pl.ds(128 * row, 128)], hw.at[row_bits(row)], hlocal.at[row]))
    for c in loads:
        c.start()
    place.greet(XY + ROW, swap=True)
    for c in loads:
        c.wait()
    drive(
        [scatter_stream(place, yw, XY, XY_ORDERS[s], (pl.ds(96 * s, 96),), yrec[s], sems)
         for s in range(4)]
        + [scatter_stream(place, hw, ROW, ROW_ORDERS[s], (pl.ds(192 * s, 192),), hrec[s], sems)
           for s in range(2)]
    )
    mine = tuple(place.bit[d] for d in XY)
    hmine = tuple(place.bit[d] for d in ROW)
    s, r = sems.take()
    swap = pltpu.make_async_remote_copy(
        src_ref=yw.at[mine], dst_ref=ybuf, send_sem=s, recv_sem=r,
        device_id=(place.row, place.aux, place.col), device_id_type=MESH)

    @pl.when(place.aux != place.row)
    def _():
        swap.start()
        swap.wait()
        out[...] = hw[hmine] - ybuf[...]

    @pl.when(place.aux == place.row)
    def _():
        out[...] = hw[hmine] - yw[mine]


def image_block(y, h):
    rows = h.shape[0]
    outs = jax.ShapeDtypeStruct((rows, 128), F32)
    scratch = [pltpu.VMEM((2, 2, 2, 2, rows, 128), F32), pltpu.VMEM((2, 2, 2, rows, 128), F32),
               pltpu.VMEM((rows, 128), F32)]
    for s in range(4):
        scratch += recv_shapes(4, (96, 128))
    for s in range(2):
        scratch += recv_shapes(3, (192, 128))
    scratch += [dma(16), dma(8), dma(23), dma(23)]
    return call(image_kernel, outs, [ANY, ANY], scratch, 1, y, h)


def scaled_kernel(g_in, ev, eo, own, rows_out, cols_out, gw, gr, gc, *rest):
    rec = [rest[4 * s: 4 * s + 4] for s in range(4)]
    local, send, recv = rest[16:]
    place = Place()
    sems = Sems(send, recv)
    loads = []
    for aux in range(8):
        for col in range(2):
            g = 2 * aux + col
            loads.append(pltpu.make_async_copy(
                g_in.at[pl.ds(320 * g, 320)], gw.at[xy_bits(aux, col)], local.at[g]))
    for c in loads:
        c.start()
    place.greet(XY + ROW)
    for c in loads:
        c.wait()
    drive(scatter_stream(place, gw, XY, XY_ORDERS[s], (pl.ds(80 * s, 80),), rec[s], sems)
          for s in range(4))
    mine = tuple(place.bit[d] for d in XY)
    rmine = tuple(place.bit[d] for d in ROW)
    scaled = gw[mine] / (ev[...] - eo[...])
    own[...] = scaled
    gr[rmine] = scaled
    gc[mine] = scaled
    drive(
        [gather_stream(place, gr, ROW, ROW_ORDERS[s][::-1], (pl.ds(160 * s, 160),), sems)
         for s in range(2)]
        + [gather_stream(place, gc, XY, XY_ORDERS[s][::-1], (pl.ds(80 * s, 80),), sems)
           for s in range(4)]
    )
    for aux in range(8):
        for col in range(2):
            cols_out[pl.ds(320 * (2 * aux + col), 320)] = gc[xy_bits(aux, col)]
    for row in range(8):
        rows_out[:, pl.ds(128 * row, 128)] = gr[row_bits(row)]


def scaled_gradient(g, ev, eo):
    outs = (jax.ShapeDtypeStruct((320, 128), F32), jax.ShapeDtypeStruct((320, 1024), F32),
            jax.ShapeDtypeStruct((5120, 128), F32))
    scratch = [pltpu.VMEM((2, 2, 2, 2, 320, 128), F32), pltpu.VMEM((2, 2, 2, 320, 128), F32),
               pltpu.VMEM((2, 2, 2, 2, 320, 128), F32)]
    for s in range(4):
        scratch += recv_shapes(4, (80, 128))
    scratch += [dma(16), dma(38), dma(38)]
    return call(scaled_kernel, outs, [ANY, VM, VM], scratch, 2, g, ev, eo)


def rotate_kernel(entries, g_in, w_in, c_in, out, gw, gfull, wfull, chalf, ghi, glo, thi, tlo,
                  tacc, whi, wlo, chi, clo, eacc, sacc, part, pbuf, *rest):
    rec = [rest[4 * s: 4 * s + 4] for s in range(4)]
    local, send, recv = rest[16:]
    place = Place()
    sems = Sems(send, recv)
    xmine = tuple(place.bit[d] for d in XY)
    rmine = tuple(place.bit[d] for d in ROW)
    loads = [
        pltpu.make_async_copy(g_in, gw, local.at[0]),
        pltpu.make_async_copy(w_in, wfull.at[rmine], local.at[1]),
        pltpu.make_async_copy(c_in.at[pl.ds(384 * place.col, 384)], chalf, local.at[2]),
    ]
    for c in loads:
        c.start()
    place.greet(XY + ROW, swap=True)
    for c in loads:
        c.wait()
    drive(scatter_stream(place, gw, XY, XY_ORDERS[s], (pl.ds(16 * s, 16),), rec[s], sems)
          for s in range(4))
    gfull[xmine + rmine] = gw[xmine]
    drive(
        [gather_stream(place, gfull, XY + ROW, ("za", "zb") + XY_ORDERS[s][::-1] + ("cc",),
                       (pl.ds(16 * s, 16),), sems) for s in range(4)]
        + [gather_stream(place, wfull, ROW, (("za", "zb", "cc"), ("zb", "za", "cc"))[s],
                         (pl.ds(192 * s, 192),), sems) for s in range(2)]
    )
    total = jnp.zeros((64, 128), F32)
    r64 = lax.broadcasted_iota(jnp.int32, (64, 128), 0)
    l128 = lax.broadcasted_iota(jnp.int32, (64, 128), 1)
    for i in range(16):
        xb = (i // 8, (i // 4) % 2, (i // 2) % 2, i % 2)
        block = gfull[xb + row_bits(i // 2)]
        total = total + jnp.where(l128 == r64 + 64 * (i % 2), block, 0.0)
    meansq = jnp.sum(total, axis=(0, 1), keepdims=True) / entries
    s1 = ROTATION_SCALE / jnp.sqrt(meansq + 1e-06)
    s2 = s1 * s1
    arow = row_bits(place.aux)
    rowl = lax.broadcasted_iota(jnp.int32, (64, 128), 0)
    for i in range(16):
        xb = (i // 8, (i // 4) % 2, (i // 2) % 2, i % 2)
        rs = pl.ds(64 * i, 64)
        for row in range(8):
            hi, lo = split(gfull[xb + row_bits(row)] * s2)
            ghi[rs, pl.ds(128 * row, 128)] = hi
            glo[rs, pl.ds(128 * row, 128)] = lo
        t_r = gfull[xb + rmine] * s2
        t_a = gfull[xb + arow] * s2
        hi, lo = split(t_r)
        thi[0, rs, pl.ds(0, 128)] = hi
        tlo[0, rs, pl.ds(0, 128)] = lo
        hi, lo = split(t_a)
        thi[0, rs, pl.ds(128, 128)] = hi
        tlo[0, rs, pl.ds(128, 128)] = lo
        eye_r = jnp.where(rowl + 64 * i == l128 + 128 * place.row, 1.0, 0.0)
        eye_a = jnp.where(rowl + 64 * i == l128 + 128 * place.aux, 1.0, 0.0)
        sacc[rs] = eye_r - t_r * (1.0 / 6.0)
        eacc[rs] = eye_a - t_a * 0.5
    coeff = [(1.0 / 120.0, 1.0 / 24.0), (-1.0 / 5040.0, -1.0 / 720.0), (0.0, 1.0 / 40320.0)]
    for k, (cs, ce) in enumerate(coeff):
        now, later = k % 2, (k + 1) % 2

        @pl.loop(0, 4)
        def _(t):
            rs = pl.ds(pl.multiple_of(t * 256, 256), 256)
            acc = jnp.dot(ghi[rs], thi[now], preferred_element_type=F32)
            acc += jnp.dot(ghi[rs], tlo[now], preferred_element_type=F32)
            acc += jnp.dot(glo[rs], thi[now], preferred_element_type=F32)
            if k < 2:
                hi, lo = split(acc)
                thi[later, rs] = hi
                tlo[later, rs] = lo
                sacc[rs] = sacc[rs] + acc[:, :128] * cs
            eacc[rs] = eacc[rs] + acc[:, 128:] * ce

    hi, lo = split(eacc[...])
    thi[0, :, pl.ds(128, 128)] = hi
    tlo[0, :, pl.ds(128, 128)] = lo
    hi, lo = split(sacc[...])
    thi[0, :, pl.ds(0, 128)] = hi
    tlo[0, :, pl.ds(0, 128)] = lo
    hi, lo = split(chalf[...])
    chi[...] = hi
    clo[...] = lo
    e_hi, e_lo = thi[0, :, pl.ds(128, 128)], tlo[0, :, pl.ds(128, 128)]
    part[...] = (jnp.dot(chi[...], e_hi, preferred_element_type=F32)
                 + jnp.dot(chi[...], e_lo, preferred_element_type=F32)
                 + jnp.dot(clo[...], e_hi, preferred_element_type=F32))
    s, r = sems.take()
    swap = pltpu.make_async_remote_copy(
        src_ref=part, dst_ref=pbuf, send_sem=s, recv_sem=r,
        device_id=(place.row, place.aux, place.col), device_id_type=MESH)

    @pl.when(place.aux != place.row)
    def _():
        swap.start()

    for row in range(8):
        hi, lo = split(wfull[row_bits(row)] * s1)
        whi[:, pl.ds(128 * row, 128)] = hi
        wlo[:, pl.ds(128 * row, 128)] = lo
    s_hi, s_lo = thi[0, :, pl.ds(0, 128)], tlo[0, :, pl.ds(0, 128)]
    out[...] = (jnp.dot(whi[...], s_hi, preferred_element_type=F32)
                + jnp.dot(whi[...], s_lo, preferred_element_type=F32)
                + jnp.dot(wlo[...], s_hi, preferred_element_type=F32))

    @pl.when(place.aux != place.row)
    def _():
        swap.wait()
        out[...] = out[...] + pbuf[...]

    @pl.when(place.aux == place.row)
    def _():
        out[...] = out[...] + part[...]


def rotate_block(entries, g, w, c_occ):
    outs = jax.ShapeDtypeStruct((384, 128), F32)
    vm = pltpu.VMEM
    scratch = [
        vm((2,) * 4 + (64, 128), F32), vm((2,) * 7 + (64, 128), F32),
        vm((2,) * 3 + (384, 128), F32), vm((384, 1024), F32),
        vm((1024, 1024), BF16), vm((1024, 1024), BF16),
        vm((2, 1024, 256), BF16), vm((2, 1024, 256), BF16), vm((1024, 256), F32),
        vm((384, 1024), BF16), vm((384, 1024), BF16),
        vm((384, 1024), BF16), vm((384, 1024), BF16),
        vm((1024, 128), F32), vm((1024, 128), F32), vm((384, 128), F32), vm((384, 128), F32),
    ]
    for s in range(4):
        scratch += recv_shapes(4, (16, 128))
    scratch += [dma(3), dma(51), dma(51)]
    return call(functools.partial(rotate_kernel, entries), outs, [ANY, ANY, ANY], scratch, 3,
                g.reshape(2, 2, 2, 2, 64, 128), w, c_occ)


def on_device(b_tensor, hcore, c_occ, c_virt, eps_occ, eps_virt):
    high = lax.Precision.HIGH
    naux, _, nocc = b_tensor.shape
    entries = float(c_virt.shape[1] * c_occ.shape[1])
    c_hi32 = lax.reduce_precision(c_occ, 8, 7)
    c_hi = c_hi32.astype(BF16)
    c_lo = (c_occ - c_hi32).astype(BF16)

    def xdot(c):
        return jnp.einsum("pmi,mj->pij", b_tensor, c, preferred_element_type=F32)

    x = (xdot(c_hi) + xdot(c_lo)).reshape(naux * nocc, -1)
    x_hi, x_lo = x_all_reduce(x)

    def ydot(v):
        return jnp.einsum("pni,pij->nj", b_tensor, v.reshape(naux, nocc, -1),
                          preferred_element_type=F32)

    y = ydot(x_hi) + ydot(x_lo)
    h = jnp.dot(hcore.T, c_occ, precision=high)
    image = image_block(y, h)
    grad = jnp.dot(c_virt.T, image, precision=high)
    own, rows, cols = scaled_gradient(grad, eps_virt[:, None], eps_occ[None, :])
    g = jnp.dot(rows.T, own, precision=high)
    w = jnp.dot(c_virt, cols, precision=high)
    return rotate_block(entries, g, w, c_occ)


def solution(mesh):
    placed = (
        P("aux", "row", "col"),
        P("row", ("aux", "col")),
        P("row", None),
        P(("aux", "col"), None),
        P("row"),
        P(("aux", "col")),
    )
    return jax.shard_map(
        on_device, mesh=mesh, in_specs=placed, out_specs=P(("aux", "col"), "row"), check_vma=False
    )
```

time: 1250 us -> 259 us (0.21)
  the two profiles are of different devices: /device:TPU:1 before, /device:TPU:16 now
where the time goes in v1:
time: 259 us
  Pallas kernels  215 us (83%)
  matrix products  40.6 us (16%)
  local copies, waits for them, and re-layouts  3.82 us (1%)
    pallas_call x4, Pallas kernels, call(): pl.pallas_call(kernel, out_shape=outs, in_specs=in_specs, out_specs=jax.t...  215 us
    dot_general x1, matrix products, on_device(): grad = jnp.dot(c_virt.T, image, precision=high)  11.2 us
    dot_general x1, matrix products, on_device(): w = jnp.dot(c_virt, cols, precision=high)  7.93 us
    dot_general x2, matrix products, xdot(): return jnp.einsum('pmi,mj->pij', b_tensor, c, preferred_element_type=F32)  7.53 us
    dot_general x2, matrix products, ydot(): jnp.einsum('pni,pij->nj', b_tensor, v.reshape(naux, nocc, -1), preferred_...  6.96 us

profile of v1, /device:TPU:16, one launch (start us, length us, event | category | flops | bytes accessed | tf_op | source)
XLA Modules:
  0.0 259.1 jit_solution(14569093643125104975)
XLA Ops:
  0.0 0.0 copy-start
  0.0 1.4 copy-done
  1.4 3.7 %fusion.5 = f32[2,512,1024]{2,1,0:T(8,128)S(1)} fusion(bf16[2,768,512]{2,1,0:T(8,128)(2,1)S(1)} %copy-done, f32[768,1024]{1,0:T(8,128)} %c_in.1), kind=kOutput, calls=%fused_computation.9 | convolution fusion | flops 1612185600 | bytes 8912896 | tf_op jit(solution)/shard_map/pmi,mj->pij/dot_general | solution.py:458
  5.2 0.0 copy-done.1
  5.2 3.8 %bitcast_add_fusion = f32[2,512,1024]{2,1,0:T(8,128)} fusion(f32[2,512,1024]{2,1,0:T(8,128)S(1)} %fusion.5, bf16[2,768,512]{2,1,0:T(8,128)(2,1)S(1)} %copy-done, f32[768,1024]{1,0:T(8,128)S(1)} %copy-done.1), kind=kOutput, calls=%fused_computation.3 | convolution fusion | flops 1614020608 | bytes 13107200 | tf_op jit(solution)/shard_map/pmi,mj->pij/dot_general | solution.py:458
  9.0 54.1 %shard_map.64 = (bf16[1024,1024]{1,0:T(8,128)(2,1)}, bf16[1024,1024]{1,0:T(8,128)(2,1)}) custom-call(f32[2,2,2,128,1024]{4,3,2,1,0:T(8,128)} %bitcast.39), custom_call_target="tpu_custom_call" | custom-call | tf_op jit(solution)/shard_map/pallas_call | solution.py:151
  63.1 0.0 copy-start.5
  63.1 3.5 %fusion.9 = f32[1024,768,1]{0,1,2:T(8,128)S(1)} fusion(bf16[2,768,512]{2,1,0:T(8,128)(2,1)S(1)} %copy-done, bf16[2,512,1024]{2,1,0:T(8,128)(2,1)} %bitcast.43), kind=kOutput, calls=%fused_computation.13 | convolution fusion | flops 1610612736 | bytes 6815744 | tf_op jit(solution)/shard_map/pni,pij->nj/dot_general | solution.py:464
  66.6 0.0 copy-done.5
  66.6 0.0 copy-start.2
  66.6 0.0 copy-start.3
  66.6 3.4 %fusion.1.y_in = f32[768,1024]{1,0:T(8,128)} fusion(f32[1024,768,1]{0,1,2:T(8,128)S(1)} %fusion.9, bf16[2,768,512]{2,1,0:T(8,128)(2,1)S(1)} %copy-done, bf16[2,512,1024]{2,1,0:T(8,128)(2,1)S(1)} %bitcast.42), kind=kOutput, calls=%fused_computation.6 | convolution fusion | flops 1611399168 | bytes 9961472 | tf_op jit(solution)/shard_map/pni,pij->nj/dot_general | solution.py:464
  70.1 0.0 copy-done.2
  70.1 0.0 copy-done.3
  70.1 3.5 %fusion.7.h_in = f32[384,1024]{1,0:T(8,128)} fusion(f32[768,384]{1,0:T(8,128)S(1)} %copy-done.3, f32[768,1024]{1,0:T(8,128)S(1)} %copy-done.2), kind=kOutput, calls=%fused_computation.11 | convolution fusion | flops 1811939328 | bytes 5898240 | tf_op jit(solution)/shard_map/dot_general | solution.py:468
  73.6 43.6 %shard_map.65 = f32[384,128]{1,0:T(8,128)} custom-call(f32[768,1024]{1,0:T(8,128)} %fusion.1.y_in, f32[384,1024]{1,0:T(8,128)} %fusion.7.h_in), custom_call_target="tpu_custom_call" | custom-call | tf_op jit(solution)/shard_map/pallas_call | solution.py:151
  117.2 0.0 copy-start.4
  117.2 11.2 %convolution_bitcast_fusion.g_in = f32[5120,128]{1,0:T(8,128)} fusion(f32[384,128]{1,0:T(8,128)} %shard_map.65, f32[384,5120]{1,0:T(8,128)} %param.9), kind=kOutput, calls=%fused_computation | convolution fusion | flops 1509949440 | bytes 10682368 | tf_op jit(solution)/shard_map/dot_general | solution.py:470
  128.4 0.8 broadcast_in_dim.8.ev
  129.2 48.2 %shard_map.66 = (f32[320,128]{1,0:T(8,128)}, f32[320,1024]{1,0:T(8,128)}, f32[5120,128]{1,0:T(8,128)}) custom-call(f32[5120,128]{1,0:T(8,128)} %convolution_bitcast_fusion.g_in, f32[320,1]{1,0:T(8,128)} %broadcast_in_dim.8.ev, f32[1,128]{1,0:T(1,128)} %bitcast.41), custom_call_target="tpu_custom_call" | custom-call | tf_op jit(solution)/shard_map/pallas_call | solution.py:151
  177.4 3.5 %fusion.8 = f32[1024,128]{1,0:T(8,128)} fusion(f32[320,1024]{1,0:T(8,128)} %get-tuple-element.12, f32[320,128]{1,0:T(8,128)} %get-tuple-element.13), kind=kOutput, calls=%fused_computation.12 | convolution fusion | flops 251658240 | bytes 1998848 | tf_op jit(solution)/shard_map/dot_general | solution.py:472
  180.9 7.9 %convolution_bitcast_fusion.1.w_in = f32[384,128]{1,0:T(8,128)} fusion(f32[5120,128]{1,0:T(8,128)} %get-tuple-element.14, f32[384,5120]{1,0:T(8,128)} %param.9), kind=kOutput, calls=%fused_computation.10 | convolution fusion | flops 1509949440 | bytes 10682368 | tf_op jit(solution)/shard_map/dot_general | solution.py:473
  188.8 68.7 %shard_map.67 = f32[384,128]{1,0:T(8,128)} custom-call(f32[2,2,2,2,64,128]{5,4,3,2,1,0:T(8,128)} %bitcast.40, f32[384,128]{1,0:T(8,128)} %convolution_bitcast_fusion.1.w_in, f32[768,1024]{1,0:T(8,128)} %c_in.1), custom_call_target="tpu_custom_call" | custom-call | tf_op jit(solution)/shard_map/pallas_call | solution.py:151
  257.5 1.6 copy.21
  (2 shorter events, 0.0 us)
Async XLA Ops:
  0.0 1.4 copy-start
  0.0 5.2 %copy-start.1 = (f32[768,1024]{1,0:T(8,128)S(1)}, f32[768,1024]{1,0:T(8,128)}, u32[]{:S(2)}) copy-start(f32[768,1024]{1,0:T(8,128)} %c_in.1) | copy-start | bytes 9437188
  63.1 3.5 %copy-start.5 = (bf16[1024,1024]{1,0:T(8,128)(2,1)S(1)}, bf16[1024,1024]{1,0:T(8,128)(2,1)}, u32[]{:S(2)}) copy-start(bf16[1024,1024]{1,0:T(8,128)(2,1)} %get-tuple-element.11) | copy-start | bytes 6291460
  66.6 3.5 %copy-start.2 = (f32[768,1024]{1,0:T(8,128)S(1)}, f32[768,1024]{1,0:T(8,128)}, u32[]{:S(2)}) copy-start(f32[768,1024]{1,0:T(8,128)} %c_in.1) | copy-start | bytes 9437188
  66.6 3.5 %copy-start.3 = (f32[768,384]{1,0:T(8,128)S(1)}, f32[768,384]{1,0:T(8,128)}, u32[]{:S(2)}) copy-start(f32[768,384]{1,0:T(8,128)} %param.7) | copy-start | bytes 3538948
  117.2 11.2 %copy-start.4 = (f32[320]{0:T(512)S(1)}, f32[320]{0:T(512)}, u32[]{:S(2)}) copy-start(f32[320]{0:T(512)} %param.11) | copy-start | bytes 3844

commit v2 on v1

v2 whole, which is shorter than its diff:
```python
import functools

import jax
import jax.numpy as jnp
from jax import lax
from jax.experimental import pallas as pl
from jax.experimental.pallas import tpu as pltpu
from jax.sharding import PartitionSpec as P

ROTATION_SCALE = 0.03
MESH = pl.DeviceIdType.MESH
F32 = jnp.float32
BF16 = jnp.bfloat16
XY = ("xa", "xb", "ya", "yb")
ROW = ("za", "zb", "cc")
VMEM_LIMIT = 60 * 1024 * 1024


class Place:
    def __init__(self):
        aux, row, col = (lax.axis_index(n) for n in ("aux", "row", "col"))
        y, xl = aux // 2, aux % 2
        z, core = row // 2, row % 2
        self.aux, self.row, self.col = aux, row, col
        self.bit = {
            "xa": (xl + col) % 2, "xb": col,
            "ya": (y + y // 2) % 2, "yb": y // 2,
            "za": (z + z // 2) % 2, "zb": z // 2,
            "cc": core,
        }
        self.partner = {
            "xa": (aux + 1 - 2 * xl, row, col),
            "xb": (aux + 1 - 2 * xl, row, 1 - col),
            "ya": (aux + 2 - 4 * (y % 2), row, col),
            "yb": (2 * (3 - y) + xl, row, col),
            "za": (aux, row + 2 - 4 * (z % 2), col),
            "zb": (aux, 2 * (3 - z) + core, col),
            "cc": (aux, row + 1 - 2 * core, col),
        }

    def greet(self, dims, swap=False):
        barrier = pltpu.get_barrier_semaphore()
        for d in dims:
            pl.semaphore_signal(barrier, inc=1, device_id=self.partner[d], device_id_type=MESH)
        if not swap:
            pl.semaphore_wait(barrier, len(dims))
            return

        @pl.when(self.aux != self.row)
        def _():
            pl.semaphore_signal(
                barrier, inc=1, device_id=(self.row, self.aux, self.col), device_id_type=MESH
            )
            pl.semaphore_wait(barrier, len(dims) + 1)

        @pl.when(self.aux == self.row)
        def _():
            pl.semaphore_wait(barrier, len(dims))


def xy_bits(aux, col):
    y, xl = aux // 2, aux % 2
    return ((xl + col) % 2, col, (y + y // 2) % 2, y // 2)


def row_bits(row):
    z, core = row // 2, row % 2
    return ((z + z // 2) % 2, z // 2, core)


class Sems:
    def __init__(self, send, recv):
        self.send, self.recv, self.n = send, recv, 0

    def take(self):
        n = self.n
        self.n += 1
        assert self.n <= self.send.shape[0]
        return self.send.at[n], self.recv.at[n]


def scatter_stream(place, work, axes, order, tail, recvs, sems):
    done = []
    for step, d in enumerate(order):
        def index(bit_of_d):
            return tuple(
                place.bit[a] if a in done else (bit_of_d if a == d else slice(None)) for a in axes
            ) + tail
        mine, theirs = index(place.bit[d]), index(1 - place.bit[d])
        s, r = sems.take()
        copy = pltpu.make_async_remote_copy(
            src_ref=work.at[theirs], dst_ref=recvs[step], send_sem=s, recv_sem=r,
            device_id=place.partner[d], device_id_type=MESH,
        )
        copy.start()
        yield
        copy.wait()
        work[mine] = work[mine] + recvs[step][...]
        done.append(d)


def gather_stream(place, full, axes, order, tail, sems):
    done = []
    for d in order:
        sl = tuple(slice(None) if a in done else place.bit[a] for a in axes) + tail
        s, r = sems.take()
        copy = pltpu.make_async_remote_copy(
            src_ref=full.at[sl], dst_ref=full.at[sl], send_sem=s, recv_sem=r,
            device_id=place.partner[d], device_id_type=MESH,
        )
        copy.start()
        yield
        copy.wait()
        done.append(d)


def drive(streams):
    streams = list(streams)
    while streams:
        alive = []
        for g in streams:
            try:
                next(g)
                alive.append(g)
            except StopIteration:
                pass
        streams = alive


def rotate(dims, k):
    return tuple(dims[k:]) + tuple(dims[:k])


XY_ORDERS = [("xa", "ya", "xb", "yb"), ("xb", "yb", "xa", "ya"),
             ("ya", "xa", "yb", "xb"), ("yb", "xb", "ya", "xa")]
ROW_ORDERS = [("cc", "za", "zb"), ("cc", "zb", "za")]


def recv_shapes(n, block):
    return [pltpu.VMEM((2,) * (n - 1 - t) + block, F32) for t in range(n)]


def dma(n):
    return pltpu.SemaphoreType.DMA((n,))


ANY = pl.BlockSpec(memory_space=pl.ANY)
VM = pl.BlockSpec(memory_space=pltpu.VMEM)


def call(kernel, outs, in_specs, scratch, cid, *args):
    return pl.pallas_call(
        kernel,
        out_shape=outs,
        in_specs=in_specs,
        out_specs=jax.tree.map(lambda _: VM, outs),
        scratch_shapes=scratch,
        compiler_params=pltpu.CompilerParams(
            collective_id=cid, has_side_effects=True, vmem_limit_bytes=VMEM_LIMIT
        ),
    )(*args)


def split(x):
    hi = x.astype(BF16)
    return hi, (x - hi.astype(F32)).astype(BF16)


PIECES = 2


def start_all(streams):
    for g in streams:
        next(g)
    return streams


def nt(a, b):
    return lax.dot_general(a, b, (((1,), (1,)), ((), ())), preferred_element_type=F32)


def nn(a, b):
    return jnp.dot(a, b, preferred_element_type=F32)


class Bag:
    def __init__(self):
        self.names, self.shapes = [], []

    def add(self, name, shape):
        self.names.append(name)
        self.shapes.append(shape)

    def recvs(self, name, n, block):
        for t, s in enumerate(recv_shapes(n, block)):
            self.add((name, t), s)

    def bind(self, refs):
        return dict(zip(self.names, refs))


def gradient_scratch():
    bag, vm = Bag(), pltpu.VMEM
    bag.add("b", vm((2, 2, 768, 512), BF16))
    bag.add("c", vm((768, 1024), F32))
    bag.add("hc", vm((768, 384), F32))
    bag.add("cth", vm((4, 2, 2, 64, 768), BF16))
    bag.add("ctl", vm((4, 2, 2, 64, 768), BF16))
    bag.add("hch", vm((768, 384), BF16))
    bag.add("hcl", vm((768, 384), BF16))
    bag.add("cv", vm((2, 384, 640), F32))
    bag.add("cvh", vm((384, 5120), BF16))
    bag.add("cvl", vm((384, 5120), BF16))
    bag.add("ev", vm((8, 640), F32))
    for p in range(PIECES):
        bag.add(("xs", p), vm((4, 64, 1024), F32))
        bag.add(("xr", p), vm((4, 64, 1024), F32))
        bag.add(("xw", p), vm((2, 2, 64, 1024), F32))
        bag.add(("xf", p), vm((2, 2, 64, 1024), F32))
        bag.add(("yw", p), vm((2, 2, 2, 2, 64, 384), F32))
        bag.add(("yb", p), vm((64, 384), F32))
        bag.add(("gw", p), vm((2, 2, 2, 2, 32, 640), F32))
        for s in range(2):
            bag.recvs(("xrec", p, s), 2, (32, 1024))
            bag.recvs(("hrec", p, s), 3, (32, 384))
        for s in range(4):
            bag.recvs(("yrec", p, s), 4, (16, 384))
            bag.recvs(("grec", p, s), 4, (8, 640))
    bag.add("hw", vm((2, 2, 2, 128, 384), F32))
    bag.add("local", dma(6))
    bag.add("send", dma(112))
    bag.add("recv", dma(112))
    return bag


def gradient_kernel(bag, b_in, h_in, c_in, cv_in, ev_in, eo, own, *refs):
    m = bag.bind(refs)
    place = Place()
    sems = Sems(m["send"], m["recv"])
    core = place.row % 2
    y, z = place.aux // 2, place.row // 2
    across = (place.aux, place.row, 1 - place.col)
    swapped = (2 * z + place.aux % 2, 2 * y + core, place.col)

    def remote(src, dst, device):
        s, r = sems.take()
        return pltpu.make_async_remote_copy(
            src_ref=src, dst_ref=dst, send_sem=s, recv_sem=r,
            device_id=device, device_id_type=MESH)

    load_c = pltpu.make_async_copy(c_in, m["c"], m["local"].at[0])
    load_b = pltpu.make_async_copy(b_in, m["b"].at[0], m["local"].at[1])
    load_h = pltpu.make_async_copy(h_in, m["hc"], m["local"].at[2])

    def load_cv(k):
        return pltpu.make_async_copy(
            cv_in.at[:, pl.ds(640 * k, 640)], m["cv"].at[k % 2], m["local"].at[3 + k % 2])

    for c in (load_c, load_b, load_h, load_cv(0), load_cv(1)):
        c.start()
    barrier = pltpu.get_barrier_semaphore()
    dims = XY + ROW
    for d in dims:
        pl.semaphore_signal(barrier, inc=1, device_id=place.partner[d], device_id_type=MESH)
    pl.semaphore_signal(barrier, inc=1, device_id=across, device_id_type=MESH)

    @pl.when(y != z)
    def _():
        pl.semaphore_signal(barrier, inc=1, device_id=swapped, device_id_type=MESH)
        pl.semaphore_wait(barrier, len(dims) + 2)

    @pl.when(y == z)
    def _():
        pl.semaphore_wait(barrier, len(dims) + 1)

    ev_copy = remote(ev_in, m["ev"], across)
    ev_copy.start()
    load_c.wait()
    for r in range(8):
        hi, lo = split(m["c"][:, pl.ds(128 * r, 128)].T)
        m["cth"][r // 2, r % 2] = hi.reshape(2, 64, 768)
        m["ctl"][r // 2, r % 2] = lo.reshape(2, 64, 768)
    load_b.wait()
    b_copy = remote(m["b"].at[0], m["b"].at[1], place.partner["cc"])

    def x_part(p, k, out):
        hi = m["cth"][:, k, p].reshape(256, 768)
        lo = m["ctl"][:, k, p].reshape(256, 768)
        for q in range(2):
            b = m["b"][0, q]
            out[..., pl.ds(512 * q, 512)] = (nn(hi, b) + nn(lo, b)).reshape(
                out.shape[:-1] + (512,))

    xc = []
    for p in range(PIECES):
        x_part(p, 1 - core, m["xs", p])
        xc.append(remote(m["xs", p], m["xr", p], place.partner["cc"]))
        xc[p].start()
        x_part(p, core, m["xw", p])
    b_copy.start()
    zaxes = ("za", "zb")
    zorders = (("za", "zb"), ("zb", "za"))
    xrs = []
    for p in range(PIECES):
        xc[p].wait()
        m["xw", p][...] = m["xw", p][...] + m["xr", p][...].reshape(2, 2, 64, 1024)
        xrs.append(start_all([
            scatter_stream(place, m["xw", p], zaxes, zorders[s], (pl.ds(32 * s, 32),),
                           [m[("xrec", p, s), t] for t in range(2)], sems)
            for s in range(2)]))

    load_h.wait()
    hi, lo = split(m["hc"][...])
    m["hch"][...] = hi
    m["hcl"][...] = lo
    for r in range(8):
        chi = m["cth"][r // 2, r % 2].reshape(128, 768)
        clo = m["ctl"][r // 2, r % 2].reshape(128, 768)
        m["hw"][row_bits(r)] = (
            nn(chi, m["hch"][...]) + nn(clo, m["hch"][...]) + nn(chi, m["hcl"][...]))
    hrs = [
        scatter_stream(place, m["hw"], ROW, ROW_ORDERS[s], (pl.ds(64 * p + 32 * s, 32),),
                       [m[("hrec", p, s), t] for t in range(3)], sems)
        for p in range(PIECES) for s in range(2)]
    start_all(hrs)

    def split_cv(k):
        load_cv(k).wait()
        hi, lo = split(m["cv"][k % 2])
        m["cvh"][:, pl.ds(640 * k, 640)] = hi
        m["cvl"][:, pl.ds(640 * k, 640)] = lo
        if k + 2 < 8:
            load_cv(k + 2).start()

    for k in range(4):
        split_cv(k)
    mine = tuple(place.bit[d] for d in zaxes)
    xag = []
    for step in range(2):
        for p in range(PIECES):
            if step == 0:
                for g in xrs[p]:
                    next(g)
            else:
                drive(xrs[p])
                m["xf", p][mine] = m["xw", p][mine]
                xag.append(start_all([
                    gather_stream(place, m["xf", p], zaxes, zorders[s][::-1],
                                  (pl.ds(32 * s, 32),), sems)
                    for s in range(2)]))
        if step == 0:
            for k in range(4, 8):
                split_cv(k)
    for p in range(PIECES):
        for g in xag[p]:
            next(g)
    yrs = []
    for p in range(PIECES):
        drive(xag[p])
        if p == 0:
            b_copy.wait()
        else:
            for g in hrs:
                next(g)
        hi, lo = split(m["xf", p][...].reshape(256, 1024))
        for side in range(2):
            xlo = core if side == 0 else 1 - core
            for half in range(2):
                rows = pl.ds(384 * half, 384)
                acc = 0.0
                for q in range(2):
                    b = m["b"][side, q, rows]
                    sl = slice(512 * q, 512 * q + 512)
                    acc = acc + nt(hi[:, sl], b) + nt(lo[:, sl], b)
                for zz in range(4):
                    m["yw", p][(xlo + half) % 2, half, (zz + zz // 2) % 2, zz // 2] = (
                        acc[64 * zz: 64 * zz + 64])
        yrs.append(start_all([
            scatter_stream(place, m["yw", p], XY, XY_ORDERS[s], (pl.ds(16 * s, 16),),
                           [m[("yrec", p, s), t] for t in range(4)], sems)
            for s in range(4)]))
    drive(hrs)
    xmine = tuple(place.bit[d] for d in XY)
    hmine = tuple(place.bit[d] for d in ROW)
    for step in range(3):
        for p in range(PIECES):
            for g in yrs[p]:
                next(g)
    swaps = []
    for p in range(PIECES):
        drive(yrs[p])
        swaps.append(remote(m["yw", p].at[xmine], m["yb", p], swapped))

        @pl.when(y != z)
        def _():
            swaps[p].start()

        @pl.when(y == z)
        def _():
            m["yb", p][...] = m["yw", p][xmine]

    grs = []
    for p in range(PIECES):
        @pl.when(y != z)
        def _():
            swaps[p].wait()

        image = m["hw"][hmine + (pl.ds(64 * p, 64),)] - m["yb", p][...]
        hi, lo = split(image)
        both = jnp.concatenate([hi, lo], axis=0)
        for aux in range(8):
            sl = pl.ds(640 * aux, 640)
            acc = nn(both, m["cvh"][:, sl])
            acc = acc[:64] + acc[64:] + nn(hi, m["cvl"][:, sl])
            for col in range(2):
                m["gw", p][xy_bits(aux, col)] = acc[32 * col: 32 * col + 32]
        grs.append(start_all([
            scatter_stream(place, m["gw", p], XY, XY_ORDERS[s], (pl.ds(8 * s, 8),),
                           [m[("grec", p, s), t] for t in range(4)], sems)
            for s in range(4)]))
    ev_copy.wait()
    for step in range(3):
        for p in range(PIECES):
            for g in grs[p]:
                next(g)
    ev = ev_in[0:1] + m["ev"][0:1]
    for p in range(PIECES):
        drive(grs[p])
        e = eo[pl.ds(64 * p + 32 * place.col, 32)]
        own[pl.ds(32 * p, 32)] = m["gw", p][xmine] / (ev - e)


def gradient_block(b, hcore, c_occ, c_virt, ev, eo):
    bag = gradient_scratch()
    return call(functools.partial(gradient_kernel, bag), jax.ShapeDtypeStruct((64, 640), F32),
                [ANY, ANY, ANY, ANY, VM, VM], bag.shapes, 0, b, hcore, c_occ, c_virt, ev, eo)


def rotate_scratch():
    bag, vm = Bag(), pltpu.VMEM
    bag.add("cv", vm((2, 384, 640), F32))
    bag.add("cvh", vm((384, 5120), BF16))
    bag.add("cvl", vm((384, 5120), BF16))
    bag.add("kc", vm((2, 2, 2, 2, 64, 640), F32))
    bag.add("kg", vm((2, 2, 2, 2, 2, 32, 384), F32))
    bag.add("win", vm((2, 32, 384), F32))
    bag.add("gw", vm((2, 2, 2, 2, 64, 128), F32))
    bag.add("gfull", vm((2,) * 7 + (64, 128), F32))
    bag.add("wfull", vm((2, 2, 2, 384, 128), F32))
    bag.add("chalf", vm((384, 1024), F32))
    for n, s in (("ghi", (1024, 1024)), ("glo", (1024, 1024)), ("thi", (2, 1024, 256)),
                 ("tlo", (2, 1024, 256)), ("whi", (384, 1024)), ("wlo", (384, 1024)),
                 ("chi", (384, 1024)), ("clo", (384, 1024))):
        bag.add(n, vm(s, BF16))
    for n, s in (("eacc", (1024, 128)), ("sacc", (1024, 128)), ("part", (384, 128)),
                 ("pbuf", (384, 128))):
        bag.add(n, vm(s, F32))
    for s in range(4):
        bag.recvs(("grec", s), 4, (16, 128))
    bag.add("local", dma(3))
    bag.add("send", dma(80))
    bag.add("recv", dma(80))
    return bag


def rotate_kernel(bag, entries, own, cv_in, c_in, out, *refs):
    m = bag.bind(refs)
    place = Place()
    sems = Sems(m["send"], m["recv"])
    col = place.col
    xmine = tuple(place.bit[d] for d in XY)
    rmine = tuple(place.bit[d] for d in ROW)
    across = (place.aux, place.row, 1 - col)
    other = (place.row, place.aux, col)

    def remote(src, dst, device):
        s, r = sems.take()
        return pltpu.make_async_remote_copy(
            src_ref=src, dst_ref=dst, send_sem=s, recv_sem=r,
            device_id=device, device_id_type=MESH)

    def load_cv(k):
        return pltpu.make_async_copy(
            cv_in.at[:, pl.ds(640 * k, 640)], m["cv"].at[k % 2], m["local"].at[k % 2])

    load_c = pltpu.make_async_copy(
        c_in.at[pl.ds(384 * col, 384)], m["chalf"], m["local"].at[2])
    for c in (load_cv(0), load_cv(1), load_c):
        c.start()
    barrier = pltpu.get_barrier_semaphore()
    dims = XY + ROW
    for d in dims:
        pl.semaphore_signal(barrier, inc=1, device_id=place.partner[d], device_id_type=MESH)
    pl.semaphore_signal(barrier, inc=1, device_id=across, device_id_type=MESH)
    m["kc"][xmine] = own[...]
    m["kg"][rmine + (slice(None), col)] = own[:, pl.ds(pl.multiple_of(256 * col, 128), 384)].reshape(2, 32, 384)
    m["win"][...] = own[:, pl.ds(pl.multiple_of(256 - 256 * col, 128), 384)].reshape(2, 32, 384)

    @pl.when(place.aux != place.row)
    def _():
        pl.semaphore_signal(barrier, inc=1, device_id=other, device_id_type=MESH)
        pl.semaphore_wait(barrier, len(dims) + 2)

    @pl.when(place.aux == place.row)
    def _():
        pl.semaphore_wait(barrier, len(dims) + 1)

    window = remote(m["win"], m["kg"].at[rmine + (slice(None), col)], across)
    window.start()
    kag = start_all([
        gather_stream(place, m["kc"], XY, XY_ORDERS[s][::-1], (pl.ds(16 * s, 16),), sems)
        for s in range(4)])

    def split_cv(k):
        load_cv(k).wait()
        hi, lo = split(m["cv"][k % 2])
        m["cvh"][:, pl.ds(640 * k, 640)] = hi
        m["cvl"][:, pl.ds(640 * k, 640)] = lo
        if k + 2 < 8:
            load_cv(k + 2).start()

    for k in range(3):
        split_cv(k)
    window.wait()
    zag = start_all([
        gather_stream(place, m["kg"], ROW, (("za", "zb", "cc"), ("zb", "za", "cc"))[s],
                      (s,), sems) for s in range(2)])
    for k in range(3, 6):
        split_cv(k)
    for step in range(2):
        for g in zag:
            next(g)
        for g in kag:
            next(g)
    for k in range(6, 8):
        split_cv(k)
    load_c.wait()
    hi, lo = split(m["chalf"][...])
    m["chi"][...] = hi
    m["clo"][...] = lo
    drive(zag)
    lanes = lax.broadcasted_iota(jnp.int32, (128, 384), 1)
    rhs = m["kg"][rmine].reshape(128, 384)
    rhs = jnp.where(lanes >= 128 * col, rhs, 0.0)
    rh, rl = split(rhs)
    for row in range(8):
        lh, ll = split(m["kg"][row_bits(row)].reshape(128, 384))
        acc = nt(lh, rh) + nt(lh, rl) + nt(ll, rh)
        for i in range(2):
            k = 2 * row + i
            m["gw"][k // 8, (k // 4) % 2, (k // 2) % 2, k % 2] = acc[64 * i: 64 * i + 64]
    grs = start_all([
        scatter_stream(place, m["gw"], XY, XY_ORDERS[s], (pl.ds(16 * s, 16),),
                       [m[("grec", s), t] for t in range(4)], sems) for s in range(4)])
    drive(grs)
    m["gfull"][xmine + rmine] = m["gw"][xmine]
    gag = start_all([
        gather_stream(place, m["gfull"], XY + ROW, ("za", "zb") + XY_ORDERS[s][::-1] + ("cc",),
                      (pl.ds(16 * s, 16),), sems) for s in range(4)])
    for g in kag:
        next(g)
    for step in range(2):
        for g in gag:
            next(g)
    drive(kag)
    w = 0.0
    for aux in range(8):
        k0 = m["kc"][xy_bits(aux, 0)]
        k1 = m["kc"][xy_bits(aux, 1)]
        kt = jnp.concatenate([k0[:32], k1[:32], k0[32:], k1[32:]], axis=0)
        kh, kl = split(kt)
        ch, cl = m["cvh"][:, pl.ds(640 * aux, 640)], m["cvl"][:, pl.ds(640 * aux, 640)]
        w = w + nt(ch, kh) + nt(ch, kl) + nt(cl, kh)
    m["wfull"][rmine] = w
    wag = start_all([
        gather_stream(place, m["wfull"], ROW, (("za", "zb", "cc"), ("zb", "za", "cc"))[s],
                      (pl.ds(192 * s, 192),), sems) for s in range(2)])
    for step in range(2):
        for g in gag:
            next(g)
        for g in wag:
            next(g)
    drive(gag)

    gfull, thi, tlo, eacc, sacc = m["gfull"], m["thi"], m["tlo"], m["eacc"], m["sacc"]
    total = jnp.zeros((64, 128), F32)
    r64 = lax.broadcasted_iota(jnp.int32, (64, 128), 0)
    l128 = lax.broadcasted_iota(jnp.int32, (64, 128), 1)
    for i in range(16):
        xb = (i // 8, (i // 4) % 2, (i // 2) % 2, i % 2)
        block = gfull[xb + row_bits(i // 2)]
        total = total + jnp.where(l128 == r64 + 64 * (i % 2), block, 0.0)
    meansq = jnp.sum(total, axis=(0, 1), keepdims=True) / entries
    s1 = ROTATION_SCALE / jnp.sqrt(meansq + 1e-06)
    s2 = s1 * s1
    arow = row_bits(place.aux)
    for i in range(16):
        xb = (i // 8, (i // 4) % 2, (i // 2) % 2, i % 2)
        rs = pl.ds(64 * i, 64)
        for row in range(8):
            hi, lo = split(gfull[xb + row_bits(row)] * s2)
            m["ghi"][rs, pl.ds(128 * row, 128)] = hi
            m["glo"][rs, pl.ds(128 * row, 128)] = lo
        t_r = gfull[xb + rmine] * s2
        t_a = gfull[xb + arow] * s2
        hi, lo = split(t_r)
        thi[0, rs, pl.ds(0, 128)] = hi
        tlo[0, rs, pl.ds(0, 128)] = lo
        hi, lo = split(t_a)
        thi[0, rs, pl.ds(128, 128)] = hi
        tlo[0, rs, pl.ds(128, 128)] = lo
        eye_r = jnp.where(r64 + 64 * i == l128 + 128 * place.row, 1.0, 0.0)
        eye_a = jnp.where(r64 + 64 * i == l128 + 128 * place.aux, 1.0, 0.0)
        sacc[rs] = eye_r - t_r * (1.0 / 6.0)
        eacc[rs] = eye_a - t_a * 0.5
    coeff = [(1.0 / 120.0, 1.0 / 24.0), (-1.0 / 5040.0, -1.0 / 720.0), (0.0, 1.0 / 40320.0)]
    for k, (cs, ce) in enumerate(coeff):
        now, later = k % 2, (k + 1) % 2

        @pl.loop(0, 4)
        def _(t):
            rs = pl.ds(pl.multiple_of(t * 256, 256), 256)
            acc = (nn(m["ghi"][rs], thi[now]) + nn(m["ghi"][rs], tlo[now])
                   + nn(m["glo"][rs], thi[now]))
            if k < 2:
                hi, lo = split(acc)
                thi[later, rs] = hi
                tlo[later, rs] = lo
                sacc[rs] = sacc[rs] + acc[:, :128] * cs
            eacc[rs] = eacc[rs] + acc[:, 128:] * ce

    e_hi, e_lo = split(eacc[...])
    m["part"][...] = nn(m["chi"][...], e_hi) + nn(m["chi"][...], e_lo) + nn(m["clo"][...], e_hi)
    swap = remote(m["part"], m["pbuf"], other)

    @pl.when(place.aux != place.row)
    def _():
        swap.start()

    drive(wag)
    for row in range(8):
        hi, lo = split(m["wfull"][row_bits(row)] * s1)
        m["whi"][:, pl.ds(128 * row, 128)] = hi
        m["wlo"][:, pl.ds(128 * row, 128)] = lo
    s_hi, s_lo = split(sacc[...])
    result = nn(m["whi"][...], s_hi) + nn(m["whi"][...], s_lo) + nn(m["wlo"][...], s_hi)

    @pl.when(place.aux != place.row)
    def _():
        swap.wait()
        out[...] = result + m["pbuf"][...]

    @pl.when(place.aux == place.row)
    def _():
        out[...] = result + m["part"][...]


def rotate_block(entries, own, c_virt, c_occ):
    bag = rotate_scratch()
    return call(functools.partial(rotate_kernel, bag, entries),
                jax.ShapeDtypeStruct((384, 128), F32), [VM, ANY, ANY], bag.shapes, 1,
                own, c_virt, c_occ)


def on_device(b_tensor, hcore, c_occ, c_virt, eps_occ, eps_virt):
    entries = float(c_virt.shape[1] * c_occ.shape[1])
    width = eps_virt.shape[0]
    ev = lax.dynamic_update_slice(
        jnp.zeros((8, 2 * width), F32), jnp.broadcast_to(eps_virt, (8, width)),
        (0, lax.axis_index("col") * width))
    own = gradient_block(b_tensor, hcore, c_occ, c_virt, ev, eps_occ[:, None])
    return rotate_block(entries, own, c_virt, c_occ)


def solution(mesh):
    placed = (
        P("aux", "row", "col"),
        P("row", ("aux", "col")),
        P("row", None),
        P(("aux", "col"), None),
        P("row"),
        P(("aux", "col")),
    )
    return jax.shard_map(
        on_device, mesh=mesh, in_specs=placed, out_specs=P(("aux", "col"), "row"), check_vma=False
    )
```

time: 259 us -> 194 us (0.75)
  matrix products: 40.6 us -> 0 us
  Pallas kernels: 215 us -> 190 us
    dot_general x8 -> x0, matrix products: 40.6 us -> none  [the longest x1 11.2 us: on_device(): grad = jnp.dot(c_virt.T, image, precision=high)]
    pallas_call x4 -> x2, Pallas kernels: 215 us -> 190 us  [call(): pl.pallas_call(kernel, out_shape=outs, in_specs=in_specs, out_specs=jax.t...]
where the time goes in v2:
time: 194 us
  Pallas kernels  190 us (98%)
  local copies, waits for them, and re-layouts  3.93 us (2%)
    pallas_call x2, Pallas kernels, call(): pl.pallas_call(kernel, out_shape=outs, in_specs=in_specs, out_specs=jax.t...  190 us

profile of v2, /device:TPU:16, one launch (start us, length us, event | category | flops | bytes accessed | tf_op | source)
XLA Modules:
  0.0 193.7 jit_solution(668481116306661712)
XLA Ops:
  0.0 0.7 broadcast_in_dim.10
  0.7 0.2 dynamic_update_slice.3.ev_in
  0.9 0.0 copy-start
  0.9 1.4 copy.7.eo
  2.3 0.0 copy-done
  2.3 98.9 %shard_map.64.own = f32[64,640]{1,0:T(8,128)} custom-call(bf16[2,768,512]{2,1,0:T(8,128)(2,1)} %b_in.1, f32[768,384]{1,0:T(8,128)} %h_in.1, f32[768,1024]{1,0:T(8,128)} %c_in.3, f32[384,5120]{1,0:T(8,128)} %cv_in.3, f32[8,640]{1,0:T(8,128)} %copy-done, f32[128,1]{1,0:T(8,128)} %copy.7.eo), custom_call_target="tpu_custom_call" | custom-call | tf_op jit(solution)/shard_map/pallas_call | solution.py:152
  101.2 90.8 %shard_map.65 = f32[384,128]{1,0:T(8,128)} custom-call(f32[64,640]{1,0:T(8,128)} %shard_map.64.own, f32[384,5120]{1,0:T(8,128)} %cv_in.3, f32[768,1024]{1,0:T(8,128)} %c_in.3), custom_call_target="tpu_custom_call" | custom-call | tf_op jit(solution)/shard_map/pallas_call | solution.py:152
  192.0 1.6 copy.10
  (1 shorter events, 0.0 us)
Async XLA Ops:
  0.9 1.4 copy-start

commit v3 on v0

v3 whole, which is shorter than its diff:
```python
import functools

import jax
import jax.numpy as jnp
from jax import lax
from jax.experimental import pallas as pl
from jax.experimental.pallas import tpu as pltpu
from jax.sharding import PartitionSpec as P

ROTATION_SCALE = 0.03
MESH = pl.DeviceIdType.MESH
F32 = jnp.float32
BF16 = jnp.bfloat16
XY = ("xa", "xb", "ya", "yb")
ROW = ("za", "zb", "cc")
VMEM_LIMIT = 62 * 1024 * 1024


class Place:
    def __init__(self):
        aux, row, col = (lax.axis_index(n) for n in ("aux", "row", "col"))
        y, xl = aux // 2, aux % 2
        z, core = row // 2, row % 2
        self.aux, self.row, self.col = aux, row, col
        self.bit = {
            "xa": (xl + col) % 2, "xb": col,
            "ya": (y + y // 2) % 2, "yb": y // 2,
            "za": (z + z // 2) % 2, "zb": z // 2,
            "cc": core,
        }
        self.partner = {
            "xa": (aux + 1 - 2 * xl, row, col),
            "xb": (aux + 1 - 2 * xl, row, 1 - col),
            "ya": (aux + 2 - 4 * (y % 2), row, col),
            "yb": (2 * (3 - y) + xl, row, col),
            "za": (aux, row + 2 - 4 * (z % 2), col),
            "zb": (aux, 2 * (3 - z) + core, col),
            "cc": (aux, row + 1 - 2 * core, col),
        }

    def greet(self, dims, swap=False):
        barrier = pltpu.get_barrier_semaphore()
        for d in dims:
            pl.semaphore_signal(barrier, inc=1, device_id=self.partner[d], device_id_type=MESH)
        if not swap:
            pl.semaphore_wait(barrier, len(dims))
            return

        @pl.when(self.aux != self.row)
        def _():
            pl.semaphore_signal(
                barrier, inc=1, device_id=(self.row, self.aux, self.col), device_id_type=MESH
            )
            pl.semaphore_wait(barrier, len(dims) + 1)

        @pl.when(self.aux == self.row)
        def _():
            pl.semaphore_wait(barrier, len(dims))


def xy_bits(aux, col):
    y, xl = aux // 2, aux % 2
    return ((xl + col) % 2, col, (y + y // 2) % 2, y // 2)


def row_bits(row):
    z, core = row // 2, row % 2
    return ((z + z // 2) % 2, z // 2, core)


class Sems:
    def __init__(self, send, recv):
        self.send, self.recv, self.n = send, recv, 0

    def take(self):
        n = self.n
        self.n += 1
        assert self.n <= self.send.shape[0]
        return self.send.at[n], self.recv.at[n]


def scatter_stream(place, work, axes, order, tail, recvs, sems):
    done = []
    for step, d in enumerate(order):
        def index(bit_of_d):
            return tuple(
                place.bit[a] if a in done else (bit_of_d if a == d else slice(None)) for a in axes
            ) + tail
        mine, theirs = index(place.bit[d]), index(1 - place.bit[d])
        s, r = sems.take()
        copy = pltpu.make_async_remote_copy(
            src_ref=work.at[theirs], dst_ref=recvs[step], send_sem=s, recv_sem=r,
            device_id=place.partner[d], device_id_type=MESH,
        )
        copy.start()
        yield
        copy.wait()
        work[mine] = work[mine] + recvs[step][...]
        done.append(d)


def gather_stream(place, full, axes, order, tail, sems):
    done = []
    for d in order:
        sl = tuple(slice(None) if a in done else place.bit[a] for a in axes) + tail
        s, r = sems.take()
        copy = pltpu.make_async_remote_copy(
            src_ref=full.at[sl], dst_ref=full.at[sl], send_sem=s, recv_sem=r,
            device_id=place.partner[d], device_id_type=MESH,
        )
        copy.start()
        yield
        copy.wait()
        done.append(d)


def drive(streams):
    streams = list(streams)
    while streams:
        alive = []
        for g in streams:
            try:
                next(g)
                alive.append(g)
            except StopIteration:
                pass
        streams = alive


def rotate(dims, k):
    return tuple(dims[k:]) + tuple(dims[:k])


XY_ORDERS = [("xa", "ya", "xb", "yb"), ("xb", "yb", "xa", "ya"),
             ("ya", "xa", "yb", "xb"), ("yb", "xb", "ya", "xa")]
ROW_ORDERS = [("cc", "za", "zb"), ("cc", "zb", "za")]


def recv_shapes(n, block):
    return [pltpu.VMEM((2,) * (n - 1 - t) + block, F32) for t in range(n)]


def dma(n):
    return pltpu.SemaphoreType.DMA((n,))


ANY = pl.BlockSpec(memory_space=pl.ANY)
VM = pl.BlockSpec(memory_space=pltpu.VMEM)


def call(kernel, outs, in_specs, scratch, cid, *args):
    return pl.pallas_call(
        kernel,
        out_shape=outs,
        in_specs=in_specs,
        out_specs=jax.tree.map(lambda _: VM, outs),
        scratch_shapes=scratch,
        compiler_params=pltpu.CompilerParams(
            collective_id=cid, has_side_effects=True, vmem_limit_bytes=VMEM_LIMIT
        ),
    )(*args)


def split(x):
    hi = x.astype(BF16)
    return hi, (x - hi.astype(F32)).astype(BF16)


def start_all(streams):
    for g in streams:
        next(g)
    return streams


def nt(a, b):
    return lax.dot_general(a, b, (((1,), (1,)), ((), ())), preferred_element_type=F32)


def nn(a, b):
    return jnp.dot(a, b, preferred_element_type=F32)


class Bag:
    def __init__(self):
        self.names, self.shapes = [], []

    def add(self, name, shape):
        self.names.append(name)
        self.shapes.append(shape)

    def recvs(self, name, n, block):
        for t, s in enumerate(recv_shapes(n, block)):
            self.add((name, t), s)

    def bind(self, refs):
        return dict(zip(self.names, refs))


PIECES = 4
R = 128 // PIECES
Q = R // 2
G_CUTS = ((0, 16), (16, 8), (24, 8), (32, 8))
G_ORDERS = [("za", "zb") + o[::-1] + ("cc",) for o in XY_ORDERS] + [XY_ORDERS[0] + ("za", "zb", "cc")]
Z_ORDERS = (("za", "zb"), ("zb", "za"))
SCHEDULE = [
    1, 2, 4, 3, 4, 6, 6, 6, 0, 1, 6, 6, 2, 3, 0, 1, 2, 3, 0, 1, 2, 3, 0, 1,
    2, 3, 1, 4, 0, 2, 5, 3, 1, 0, 4, 2, 3, 1, 0, 2, 3, 1, 0, 2, 5, 3, 0, 4,
    1, 2, 3, 0, 1, 5, 2, 3, 5, 0, 1, 2, 3, 0, 1, 2, 3, 0, 1, 2, 3, 0, 8, 9,
    1, 2, 10, 3, 7, 0, 1, 8, 2, 9, 3, 10, 0, 7, 1, 2, 1, 3, 2, 0, 3, 0, 8, 7,
    9, 10, 12, 12, 12, 12, 12, 12, 8, 7, 9, 10, 11, 11, 11, 11, 12, 12, 11, 12, 11, 12, 11, 12,
]


def grad_cuts(p):
    return [((slice(None), pl.ds(128 * s, 128)), XY_ORDERS[s if s < 4 else p]) for s in range(5)]


def scratch():
    bag, vm = Bag(), pltpu.VMEM
    bag.add("b", vm((2, 2, 768, 512), BF16))
    bag.add("c", vm((768, 1024), F32))
    bag.add("cg", vm((384, 1024), F32))
    bag.add("hc", vm((768, 384), F32))
    bag.add("ct", vm((2, PIECES, 2, 4, R, 768), BF16))
    bag.add("hch", vm((768, 384), BF16))
    bag.add("hcl", vm((768, 384), BF16))
    bag.add("cv", vm((2, 384, 256), F32))
    bag.add("cvh", vm((384, 5120), BF16))
    bag.add("cvl", vm((384, 5120), BF16))
    bag.add("ev", vm((2, 8, 640), F32))
    bag.add("eo", vm((128, 8), F32))
    for p in range(PIECES):
        bag.add(("xs", p), vm((4, R, 1024), F32))
        bag.add(("xr", p), vm((4, R, 1024), F32))
        bag.add(("xw", p), vm((2, 2, R, 1024), F32))
        bag.add(("xf", p), vm((2, 2, R, 1024), F32))
        bag.add(("yw", p), vm((2, 2, 2, 2, R, 384), F32))
        bag.add(("yb", p), vm((R, 384), F32))
        bag.add(("gw", p), vm((2, 2, 2, 2, Q, 640), F32))
        for s in range(2):
            bag.recvs(("xrec", p, s), 2, (R // 2, 1024))
        for s in range(4):
            bag.recvs(("yrec", p, s), 4, (R // 4, 384))
        for s in range(5):
            bag.recvs(("grec", p, s), 4, (Q, 128))
    for s in range(2):
        bag.recvs(("hrec", s), 3, (64, 384))
    bag.add("hw", vm((2, 2, 2, 128, 384), F32))
    bag.add("kc", vm((2, 2, 2, 2, PIECES, Q, 640), F32))
    bag.add("kg", vm((2, 2, 2, PIECES, 2, Q, 384), F32))
    bag.add("win", vm((PIECES, Q, 384), F32))
    bag.add("gs", vm((2, 2, 2, 2, 40, 128), F32))
    for s, (_, n) in enumerate(G_CUTS):
        bag.recvs(("gsrec", s), 4, (n, 128))
    bag.add("gfull", vm((2,) * 7 + (40, 128), F32))
    bag.add("wfull", vm((2, 2, 2, 384, 128), F32))
    bag.add("ghi", vm((1024, 1024), BF16))
    bag.add("glo", vm((1024, 1024), BF16))
    bag.add("t", vm((2, 1024, 256), BF16))
    bag.add("acc", vm((2, 1024, 128), F32))
    bag.add("local", dma(12))
    bag.add("send", dma(320))
    bag.add("recv", dma(320))
    return bag


def kernel(bag, entries, b_in, h_in, c_in, cv_in, ev_in, eo_in, out, *refs):
    m = bag.bind(refs)
    place = Place()
    sems = Sems(m["send"], m["recv"])
    core, col = place.row % 2, place.col
    other = 1 - core
    y, z = place.aux // 2, place.row // 2
    across = (place.aux, place.row, 1 - col)
    swapped = (2 * z + place.aux % 2, 2 * y + core, col)
    xmine = tuple(place.bit[d] for d in XY)
    rmine = tuple(place.bit[d] for d in ROW)
    zmine = rmine[:2]

    def remote(src, dst, device):
        s, r = sems.take()
        return pltpu.make_async_remote_copy(
            src_ref=src, dst_ref=dst, send_sem=s, recv_sem=r,
            device_id=device, device_id_type=MESH)

    def load_c(k, zz):
        sl = pl.ds(pl.multiple_of(128 * (2 * zz + k), 128), 128)
        which = zz if k is core else 4 + zz
        return pltpu.make_async_copy(c_in.at[:, sl], m["c"].at[:, sl], m["local"].at[which])

    load_b = pltpu.make_async_copy(b_in, m["b"].at[0], m["local"].at[8])
    load_h = pltpu.make_async_copy(h_in, m["hc"], m["local"].at[9])

    def load_cv(k):
        return pltpu.make_async_copy(
            cv_in.at[:, pl.ds(256 * k, 256)], m["cv"].at[k % 2], m["local"].at[10 + k % 2])

    for zz in range(4):
        load_c(other, zz).start()
    load_b.start()
    for zz in range(4):
        load_c(core, zz).start()
    barrier = pltpu.get_barrier_semaphore()
    dims = XY + ROW
    for d in dims:
        pl.semaphore_signal(barrier, inc=1, device_id=place.partner[d], device_id_type=MESH)
    pl.semaphore_signal(barrier, inc=1, device_id=across, device_id_type=MESH)

    @pl.when(y != z)
    def _():
        pl.semaphore_signal(barrier, inc=1, device_id=swapped, device_id_type=MESH)

    def turn_c(k, zz):
        load_c(k, zz).wait()
        sl = pl.ds(pl.multiple_of(128 * (2 * zz + k), 128), 128)
        hi, lo = split(m["c"][:, sl].T)
        m["ct"][k, :, 0, zz] = hi.reshape(PIECES, R, 768)
        m["ct"][k, :, 1, zz] = lo.reshape(PIECES, R, 768)

    def x_part(p, k, out_ref):
        both = m["ct"][k, p].reshape(8 * R, 768)
        for q in range(2):
            acc = nn(both, m["b"][0, q])
            out_ref[..., pl.ds(512 * q, 512)] = (acc[:4 * R] + acc[4 * R:]).reshape(
                out_ref.shape[:-1] + (512,))

    for zz in range(4):
        turn_c(other, zz)
    load_b.wait()
    x_part(0, other, m["xs", 0])

    @pl.when(y != z)
    def _():
        pl.semaphore_wait(barrier, len(dims) + 2)

    @pl.when(y == z)
    def _():
        pl.semaphore_wait(barrier, len(dims) + 1)

    xc = [remote(m["xs", p], m["xr", p], place.partner["cc"]) for p in range(PIECES)]
    xc[0].start()
    load_h.start()
    load_cv(0).start()
    load_cv(1).start()
    for zz in range(4):
        turn_c(core, zz)
    b_copy = remote(m["b"].at[0], m["b"].at[1], place.partner["cc"])
    ev_copy = remote(m["ev"].at[0], m["ev"].at[1], across)
    for p in range(PIECES):
        x_part(p, core, m["xw", p])
        if p + 1 < PIECES:
            x_part(p + 1, other, m["xs", p + 1])
            xc[p + 1].start()
    b_copy.start()

    tasks, finished, have_b = {}, set(), []

    def advance(n):
        if n in tasks:
            try:
                next(tasks[n])
            except StopIteration:
                del tasks[n]
                finished.add(n)

    def complete(n):
        while n in tasks:
            advance(n)

    def launch(n, g):
        tasks[n] = g
        advance(n)

    def steps(streams, n):
        for _ in range(n - 1):
            yield
            for g in streams:
                next(g)
        yield
        drive(streams)

    def piece(p):
        yield
        xc[p].wait()
        m["xw", p][...] = m["xw", p][...] + m["xr", p][...].reshape(2, 2, R, 1024)
        streams = start_all([
            scatter_stream(place, m["xw", p], ("za", "zb"), Z_ORDERS[s],
                           (pl.ds(R // 2 * s, R // 2),),
                           [m[("xrec", p, s), t] for t in range(2)], sems) for s in range(2)])
        yield from steps(streams, 2)
        m["xf", p][zmine] = m["xw", p][zmine]
        streams = start_all([
            gather_stream(place, m["xf", p], ("za", "zb"), Z_ORDERS[s][::-1],
                          (pl.ds(R // 2 * s, R // 2),), sems) for s in range(2)])
        yield from steps(streams, 2)
        if not have_b:
            b_copy.wait()
            have_b.append(p)
        hi, lo = split(m["xf", p][...].reshape(4 * R, 1024))
        both = jnp.concatenate([hi, lo], axis=0)
        for side in range(2):
            xlo = core if side == 0 else other
            for half in range(2):
                rows = pl.ds(384 * half, 384)
                acc = nt(both[:, :512], m["b"][side, 0, rows])
                acc += nt(both[:, 512:], m["b"][side, 1, rows])
                acc = acc[:4 * R] + acc[4 * R:]
                for zz in range(4):
                    m["yw", p][(xlo + half) % 2, half, (zz + zz // 2) % 2, zz // 2] = (
                        acc[R * zz: R * zz + R])
        streams = start_all([
            scatter_stream(place, m["yw", p], XY, XY_ORDERS[s], (pl.ds(R // 4 * s, R // 4),),
                           [m[("yrec", p, s), t] for t in range(4)], sems) for s in range(4)])
        yield from steps(streams, 4)
        swap = remote(m["yw", p].at[xmine], m["yb", p], swapped)

        @pl.when(y != z)
        def _():
            swap.start()

        @pl.when(y == z)
        def _():
            m["yb", p][...] = m["yw", p][xmine]

        yield
        complete(4)
        complete(6)

        @pl.when(y != z)
        def _():
            swap.wait()

        image = m["hw"][rmine + (pl.ds(R * p, R),)] - m["yb", p][...]
        hi, lo = split(image)
        both = jnp.concatenate([hi, lo], axis=0)
        for aux in range(8):
            sl = pl.ds(640 * aux, 640)
            acc = nn(both, m["cvh"][:, sl])
            acc = acc[:R] + acc[R:] + nn(hi, m["cvl"][:, sl])
            for c in range(2):
                m["gw", p][xy_bits(aux, c)] = acc[Q * c: Q * c + Q]
        streams = start_all([
            scatter_stream(place, m["gw", p], XY, order, tail,
                           [m[("grec", p, s), t] for t in range(4)], sems)
            for s, (tail, order) in enumerate(grad_cuts(p))])
        yield from steps(streams, 4)
        ev = m["ev"][0, 0:1] + m["ev"][1, 0:1]
        eo = m["eo"][pl.ds(R * p + Q * col, Q), 0:1]
        m["kc"][xmine + (p,)] = m["gw", p][xmine] / (ev - eo)
        mine = pl.ds(pl.multiple_of(256 * col, 128), 384)
        theirs = pl.ds(pl.multiple_of(256 - 256 * col, 128), 384)
        m["kg"][rmine + (p, col)] = m["kc"][xmine + (p, slice(None), mine)]
        m["win"][p] = m["kc"][xmine + (p, slice(None), theirs)]
        window = remote(m["win"].at[p], m["kg"].at[rmine + (p, col)], across)
        window.start()
        launch(7 + p, gather_piece(p))
        yield
        window.wait()
        streams = start_all([
            gather_stream(place, m["kg"], ROW, Z_ORDERS[s] + ("cc",), (p, s), sems)
            for s in range(2)])
        yield from steps(streams, 3)

    def gather_piece(p):
        yield from steps(start_all([
            gather_stream(place, m["kc"], XY, XY_ORDERS[p][::-1], (p,), sems)]), 4)

    def h_task():
        yield
        load_h.wait()
        hi, lo = split(m["hc"][...])
        m["hch"][...] = hi
        m["hcl"][...] = lo
        for r in range(8):
            chi = m["ct"][r % 2, :, 0, r // 2].reshape(128, 768)
            clo = m["ct"][r % 2, :, 1, r // 2].reshape(128, 768)
            m["hw"][row_bits(r)] = (
                nn(chi, m["hch"][...]) + nn(clo, m["hch"][...]) + nn(chi, m["hcl"][...]))
            if r == 3:
                yield
        yield from steps(start_all([
            scatter_stream(place, m["hw"], ROW, ROW_ORDERS[s], (pl.ds(64 * s, 64),),
                           [m[("hrec", s), t] for t in range(3)], sems) for s in range(2)]), 3)

    def c_rows():
        source = row_bits(place.aux)
        yield

        @pl.when(place.aux == place.row)
        def _():
            m["cg"][...] = m["c"][pl.ds(pl.multiple_of(384 * col, 384), 384)]

        differs = {d: (place.bit[d] - source[ROW.index(d)]) * (place.bit[d] - source[ROW.index(d)])
                   for d in ROW}
        for k in range(3):
            copies = []
            for s in range(2):
                order = Z_ORDERS[s] + ("cc",)
                later = sum((differs[d] for d in order[k + 1:]), 0)
                at = m["cg"].at[pl.ds(192 * s, 192)]
                copy = remote(at, at, place.partner[order[k]])
                sends = later + differs[order[k]] == 0
                takes = later + (1 - differs[order[k]]) == 0
                copies.append((copy, sends, takes))

                @pl.when(sends)
                def _():
                    copy.start()

            yield
            for copy, sends, takes in copies:
                @pl.when(sends)
                def _():
                    copy.wait_send()

                @pl.when(takes)
                def _():
                    copy.wait_recv()

    def cv_task():
        m["ev"][0] = jnp.zeros((8, 640), F32)
        value = jnp.broadcast_to(ev_in[...], (8, 320))

        @pl.when(col == 0)
        def _():
            m["ev"][0, :, :320] = value

        @pl.when(col == 1)
        def _():
            m["ev"][0, :, 320:] = value

        ev_copy.start()
        m["eo"][...] = jnp.broadcast_to(eo_in[...], (8, 128)).T
        for k in range(20):
            if k % 4 == 0:
                yield
            load_cv(k).wait()
            hi, lo = split(m["cv"][k % 2])
            m["cvh"][:, pl.ds(256 * k, 256)] = hi
            m["cvl"][:, pl.ds(256 * k, 256)] = lo
            if k + 2 < 20:
                load_cv(k + 2).start()
        ev_copy.wait()

    def w_task():
        w = 0.0
        for aux in range(8):
            if aux % 2 == 0:
                yield
            k0 = m["kc"][xy_bits(aux, 0)]
            k1 = m["kc"][xy_bits(aux, 1)]
            kh, kl = split(jnp.concatenate([k0[:, None], k1[:, None]], axis=1).reshape(128, 640))
            ch, cl = m["cvh"][:, pl.ds(640 * aux, 640)], m["cvl"][:, pl.ds(640 * aux, 640)]
            both = nt(ch, jnp.concatenate([kh, kl], axis=0))
            w = w + both[:, :128] + both[:, 128:] + nt(cl, kh)
        m["wfull"][rmine] = w
        yield from steps(start_all([
            gather_stream(place, m["wfull"], ROW, Z_ORDERS[s] + ("cc",),
                          (pl.ds(192 * s, 192),), sems) for s in range(2)]), 3)

    def place_blocks(r):
        chunks = [m["gfull"][(i // 8, (i // 4) % 2, (i // 2) % 2, i % 2) + row_bits(r)]
                  for i in range(16)]
        column = jnp.concatenate(chunks, axis=0)
        for k in range(5):
            block = column[128 * k: 128 * k + 128]
            i = (r + k) % 8
            hi, lo = split(block)
            m["ghi"][pl.ds(128 * i, 128), pl.ds(128 * r, 128)] = hi
            m["glo"][pl.ds(128 * i, 128), pl.ds(128 * r, 128)] = lo
            if 0 < k < 4:
                hi, lo = split(block.T)
                m["ghi"][pl.ds(128 * r, 128), pl.ds(128 * i, 128)] = hi
                m["glo"][pl.ds(128 * r, 128), pl.ds(128 * i, 128)] = lo
        return column[:128]

    def g_task():
        lanes = lax.broadcasted_iota(jnp.int32, (128, 384), 1)
        rhs = m["kg"][rmine].reshape(128, 384)
        rh, rl = split(jnp.where(lanes >= 128 * col, rhs, 0.0))
        accs = []
        for k in range(5):
            lh, ll = split(m["kg"][row_bits((place.row + k) % 8)].reshape(128, 384))
            accs.append(nt(lh, rh) + nt(lh, rl) + nt(ll, rh))
        acc = jnp.concatenate(accs, axis=0)
        for k in range(16):
            m["gs"][k // 8, (k // 4) % 2, (k // 2) % 2, k % 2] = acc[40 * k: 40 * k + 40]
        yield from steps(start_all([
            scatter_stream(place, m["gs"], XY, XY_ORDERS[s], (pl.ds(*cut),),
                           [m[("gsrec", s), t] for t in range(4)], sems)
            for s, cut in enumerate(G_CUTS)]), 4)
        m["gfull"][xmine + rmine] = m["gs"][xmine]
        yield from steps(start_all([
            gather_stream(place, m["gfull"], XY + ROW, G_ORDERS[s], (pl.ds(8 * s, 8),), sems)
            for s in range(5)]), 7)

    for p in range(PIECES):
        launch(p, piece(p))
    launch(4, h_task())
    launch(5, c_rows())
    launch(6, cv_task())

    def follow():
        if 12 not in tasks and 12 not in finished and finished.issuperset(range(PIECES)):
            launch(12, g_task())
        if 11 not in tasks and 11 not in finished and finished.issuperset(range(7, 7 + PIECES)):
            launch(11, w_task())

    for n in SCHEDULE:
        advance(n)
        follow()
    while tasks:
        for n in sorted(tasks):
            advance(n)
        follow()

    ghi, glo, t, acc_ref = m["ghi"], m["glo"], m["t"], m["acc"]
    r128 = lax.broadcasted_iota(jnp.int32, (128, 128), 0)
    l128 = lax.broadcasted_iota(jnp.int32, (128, 128), 1)
    total = jnp.zeros((128, 128), F32)
    for r in range(8):
        total = total + jnp.where(r128 == l128, place_blocks(r), 0.0)
    meansq = jnp.sum(total, axis=(0, 1), keepdims=True) / entries
    s1 = ROTATION_SCALE / jnp.sqrt(meansq + 1e-06)
    s2 = s1 * s1
    at = pl.ds(pl.multiple_of(128 * place.row, 128), 128)
    t[0, :, :128] = ghi[:, at]
    t[0, :, 128:] = glo[:, at]
    rows8 = lax.broadcasted_iota(jnp.int32, (1024, 128), 0)
    lanes8 = lax.broadcasted_iota(jnp.int32, (1024, 128), 1)
    g1 = (ghi[:, at].astype(F32) + glo[:, at].astype(F32)) * s2
    eye = jnp.where(rows8 == lanes8 + 128 * place.row, 1.0, 0.0)
    acc_ref[0] = eye - g1 * 0.5
    acc_ref[1] = eye - g1 * (1.0 / 6.0)
    coeff = [(1.0 / 24.0, 1.0 / 120.0), (-1.0 / 720.0, -1.0 / 5040.0), (1.0 / 40320.0, 0.0)]
    for k, (ce, cs) in enumerate(coeff):
        now, later = k % 2, (k + 1) % 2
        scale = s2 * s2 if k == 0 else s2

        @pl.loop(0, 4)
        def _(i):
            rs = pl.ds(pl.multiple_of(i * 256, 256), 256)
            high = nn(ghi[rs], t[now])
            power = (high[:, :128] + high[:, 128:] + nn(glo[rs], t[now, :, :128])) * scale
            if k < 2:
                hi, lo = split(power)
                t[later, rs, :128] = hi
                t[later, rs, 128:] = lo
                acc_ref[1, rs] = acc_ref[1, rs] + power * cs
            acc_ref[0, rs] = acc_ref[0, rs] + power * ce

    e_hi, e_lo = split(acc_ref[0])
    c_hi, c_lo = split(m["cg"][...])
    both = nn(c_hi, jnp.concatenate([e_hi, e_lo], axis=1))
    result = both[:, :128] + both[:, 128:] + nn(c_lo, e_hi)
    s_hi, s_lo = split(acc_ref[1] * s1)
    w_all = jnp.concatenate([m["wfull"][row_bits(r)] for r in range(8)], axis=1)
    w_hi, w_lo = split(w_all)
    both = nn(w_hi, jnp.concatenate([s_hi, s_lo], axis=1))
    out[...] = result + both[:, :128] + both[:, 128:] + nn(w_lo, s_hi)


def on_device(b_tensor, hcore, c_occ, c_virt, eps_occ, eps_virt):
    entries = float(c_virt.shape[1] * c_occ.shape[1])
    bag = scratch()
    return call(functools.partial(kernel, bag, entries), jax.ShapeDtypeStruct((384, 128), F32),
                [ANY, ANY, ANY, ANY, VM, VM], bag.shapes, 0,
                b_tensor, hcore, c_occ, c_virt, eps_virt[None, :], eps_occ[None, :])


def solution(mesh):
    placed = (
        P("aux", "row", "col"),
        P("row", ("aux", "col")),
        P("row", None),
        P(("aux", "col"), None),
        P("row"),
        P(("aux", "col")),
    )
    return jax.shard_map(
        on_device, mesh=mesh, in_specs=placed, out_specs=P(("aux", "col"), "row"), check_vma=False
    )
```

time: 1250 us -> 166 us (0.13)
  waiting for transfers between devices: 1080 us -> 0 us
  Pallas kernels: 0 us -> 162 us
  blocking collectives: 70.2 us -> 0 us
  matrix products: 65.7 us -> 0 us
  between operations: 14 us -> 0.01 us
    reduce_scatter x3 -> x0, waiting for transfers between devices: 507 us -> none  [the longest x1 395 us: on_device(): lax.psum_scatter(terms, ('aux', 'col'), scatter_dimension=1, tiled=True)]
    psum x5 -> x0, waiting for transfers between devices: 397 us -> none  [the longest x4 338 us: occ_partial(): return lax.psum(local_term, ('aux', 'col'))]
    all_gather x3 -> x0, waiting for transfers between devices: 174 us -> none  [the longest x1 79 us: on_device(): lax.all_gather(virt_sum, ('aux', 'col'), axis=0, tiled=True)]
    pallas_call x0 -> x1, Pallas kernels: none -> 162 us  [call(): pl.pallas_call(kernel, out_shape=outs, in_specs=in_specs, out_specs=jax.t...]
    psum x1 -> x0, blocking collectives: 70.2 us -> none  [on_device(): meansq = lax.psum(jnp.sum(scaled * scaled), ('aux', 'row', 'col')) / (V * O)]
    dot_general x12 -> x0, matrix products: 65.7 us -> none  [the longest x1 16.5 us: on_device(): jnp.einsum('pmi,pni->mn', b_tensor, lax.all_gather(b_tensor, 'row', axis=...]
  transfers between devices with their start and end apart: 11 -> 0, of which waited for: 11 -> 0; matrix products, arithmetic and copies ran while one was open for 1% -> 0% of each run, Pallas kernels for 0% -> 0%
where the time goes in v3:
time: 166 us; the launch traced here: 165 us
  Pallas kernels  162 us (98%)
  local copies, waits for them, and re-layouts  2.86 us (2%)
    pallas_call x1, Pallas kernels, call(): pl.pallas_call(kernel, out_shape=outs, in_specs=in_specs, out_specs=jax.t...  162 us

profile of v3, /device:TPU:1, one launch (start us, length us, event | category | flops | bytes accessed | tf_op | source)
XLA Modules:
  0.0 165.3 jit_solution(12613900808807851898)
XLA Ops:
  0.0 1.2 broadcast_in_dim.6.ev_in
  1.2 162.5 %shard_map.64 = f32[384,128]{1,0:T(8,128)} custom-call(bf16[2,768,512]{2,1,0:T(8,128)(2,1)} %b_in.1, f32[768,384]{1,0:T(8,128)} %h_in.1, f32[768,1024]{1,0:T(8,128)} %c_in.1, f32[384,5120]{1,0:T(8,128)} %cv_in.1, f32[1,320]{1,0:T(1,128)} %broadcast_in_dim.6.ev_in, f32[1,128]{1,0:T(1,128)} %bitcast.1), custom_call_target="tpu_custom_call" | custom-call | tf_op jit(solution)/shard_map/pallas_call | solution.py:152
  163.7 1.6 copy.8

commit v4 on v3

--- a/solution.py
+++ b/solution.py
@@ -196,6 +196,52 @@
         return dict(zip(self.names, refs))
 
 
+LIMIT = 16383.0
+
+
+def pack(parts):
+    peak = jnp.max(jnp.abs(parts[0]), axis=0)
+    for v in parts[1:]:
+        peak = jnp.maximum(peak, jnp.max(jnp.abs(v), axis=0))
+    peak = jnp.maximum(peak, 1e-30)
+    n = [jnp.round(v * (LIMIT / peak)) for v in parts]
+    h3, h4 = jnp.floor(n[3] * (1 / 32)), jnp.floor(n[4] * (1 / 32))
+    words = [n[0] * 1024 + h3, n[1] * 1024 + h4,
+             n[2] * 1024 + ((n[3] - 32 * h3) * 32 + (n[4] - 32 * h4) - 512)]
+    if len(parts) == 8:
+        h = jnp.floor(n[7] * (1 / 128))
+        words += [n[5] * 256 + h, n[6] * 256 + (n[7] - 128 * h)]
+    return peak * (1 / LIMIT), words
+
+
+def unpack(scale, words):
+    top = [jnp.floor((w + 512) * (1 / 1024)) for w in words[:3]]
+    h3, h4, rest = (w - 1024 * t for w, t in zip(words, top))
+    rest = rest + 512
+    l3 = jnp.floor(rest * (1 / 32))
+    n = top + [h3 * 32 + l3, h4 * 32 + (rest - 32 * l3)]
+    if len(words) == 5:
+        n5 = jnp.floor((words[3] + 128) * (1 / 256))
+        n6 = jnp.floor(words[4] * (1 / 256))
+        n += [n5, n6, (words[3] - 256 * n5) * 128 + (words[4] - 256 * n6)]
+    return [v * scale for v in n]
+
+
+def pack_into(ref, block):
+    k = block.shape[-1] // 128
+    block = block.reshape(-1, 8, block.shape[-1])
+    m = block.shape[0]
+    scale, words = pack([block[..., 128 * i: 128 * i + 128] for i in range(k)])
+    ref[0] = scale
+    for j, w in enumerate(words):
+        ref[1 + j * m: 1 + (j + 1) * m] = w
+
+
+def unpack_from(wire, m):
+    words = [wire[1 + j * m: 1 + (j + 1) * m] for j in range((wire.shape[0] - 1) // m)]
+    return unpack(wire[0], words)
+
+
 PIECES = 4
 R = 128 // PIECES
 Q = R // 2
@@ -203,11 +249,11 @@
 G_ORDERS = [("za", "zb") + o[::-1] + ("cc",) for o in XY_ORDERS] + [XY_ORDERS[0] + ("za", "zb", "cc")]
 Z_ORDERS = (("za", "zb"), ("zb", "za"))
 SCHEDULE = [
-    1, 2, 4, 3, 4, 6, 6, 6, 0, 1, 6, 6, 2, 3, 0, 1, 2, 3, 0, 1, 2, 3, 0, 1,
-    2, 3, 1, 4, 0, 2, 5, 3, 1, 0, 4, 2, 3, 1, 0, 2, 3, 1, 0, 2, 5, 3, 0, 4,
-    1, 2, 3, 0, 1, 5, 2, 3, 5, 0, 1, 2, 3, 0, 1, 2, 3, 0, 1, 2, 3, 0, 8, 9,
-    1, 2, 10, 3, 7, 0, 1, 8, 2, 9, 3, 10, 0, 7, 1, 2, 1, 3, 2, 0, 3, 0, 8, 7,
-    9, 10, 12, 12, 12, 12, 12, 12, 8, 7, 9, 10, 11, 11, 11, 11, 12, 12, 11, 12, 11, 12, 11, 12,
+    0, 4, 1, 3, 4, 0, 2, 6, 6, 1, 6, 6, 3, 6, 0, 2, 1, 3, 0, 2, 1, 3, 0, 2,
+    1, 3, 0, 2, 1, 4, 3, 0, 2, 1, 3, 0, 4, 2, 1, 3, 0, 5, 2, 1, 3, 4, 2, 0,
+    1, 3, 2, 0, 5, 1, 3, 2, 0, 1, 3, 2, 0, 1, 3, 2, 0, 1, 5, 3, 2, 7, 8, 0,
+    5, 10, 1, 9, 3, 2, 7, 0, 8, 1, 10, 3, 9, 2, 0, 7, 1, 8, 0, 3, 10, 1, 2, 9,
+    3, 2, 12, 12, 12, 7, 8, 9, 12, 10, 11, 11, 11, 12, 11, 12, 11, 12, 12, 11, 12, 11, 12, 12,
 ]
 
 
@@ -238,7 +284,10 @@
         bag.add(("yb", p), vm((R, 384), F32))
         bag.add(("gw", p), vm((2, 2, 2, 2, Q, 640), F32))
         for s in range(2):
-            bag.recvs(("xrec", p, s), 2, (R // 2, 1024))
+            for t, tiles in enumerate((4, 2)):
+                bag.add(("xout", p, s, t), vm((5 * tiles + 1, 8, 128), F32))
+                bag.add(("xin", p, s, t), vm((5 * tiles + 1, 8, 128), F32))
+            bag.add(("xg", p, s), vm((2, 2, 11, 8, 128), F32))
         for s in range(4):
             bag.recvs(("yrec", p, s), 4, (R // 4, 384))
         for s in range(5):
@@ -246,7 +295,8 @@
     for s in range(2):
         bag.recvs(("hrec", s), 3, (64, 384))
     bag.add("hw", vm((2, 2, 2, 128, 384), F32))
-    bag.add("kc", vm((2, 2, 2, 2, PIECES, Q, 640), F32))
+    bag.add("kc", vm((2, 2, 2, 2, PIECES, 7, 8, 128), F32))
+    bag.add("own", vm((PIECES, Q, 640), F32))
     bag.add("kg", vm((2, 2, 2, PIECES, 2, Q, 384), F32))
     bag.add("win", vm((PIECES, Q, 384), F32))
     bag.add("gs", vm((2, 2, 2, 2, 40, 128), F32))
@@ -379,20 +429,40 @@
         yield
         drive(streams)
 
+    def x_scatter(p, s):
+        work, rows, done = m["xw", p], pl.ds(16 * s, 16), []
+        for t, d in enumerate(Z_ORDERS[s]):
+            def index(bit):
+                return tuple(place.bit[a] if a in done else (bit if a == d else slice(None))
+                             for a in ("za", "zb")) + (rows,)
+            mine, theirs = index(place.bit[d]), index(1 - place.bit[d])
+            pack_into(m["xout", p, s, t], work[theirs])
+            copy = remote(m["xout", p, s, t], m["xin", p, s, t], place.partner[d])
+            copy.start()
+            yield
+            copy.wait()
+            for k, v in enumerate(unpack_from(m["xin", p, s, t][...], (4, 2)[t])):
+                at = mine + (pl.ds(128 * k, 128),)
+                work[at] = work[at] + v.reshape((2, 16, 128) if t == 0 else (16, 128))
+            done.append(d)
+
     def piece(p):
         yield
         xc[p].wait()
         m["xw", p][...] = m["xw", p][...] + m["xr", p][...].reshape(2, 2, R, 1024)
+        streams = start_all([x_scatter(p, s) for s in range(2)])
+        yield from steps(streams, 2)
+        for s in range(2):
+            pack_into(m["xg", p, s].at[zmine], m["xw", p][zmine + (pl.ds(16 * s, 16),)])
         streams = start_all([
-            scatter_stream(place, m["xw", p], ("za", "zb"), Z_ORDERS[s],
-                           (pl.ds(R // 2 * s, R // 2),),
-                           [m[("xrec", p, s), t] for t in range(2)], sems) for s in range(2)])
+            gather_stream(place, m["xg", p, s], ("za", "zb"), Z_ORDERS[s][::-1], (), sems)
+            for s in range(2)])
         yield from steps(streams, 2)
-        m["xf", p][zmine] = m["xw", p][zmine]
-        streams = start_all([
-            gather_stream(place, m["xf", p], ("za", "zb"), Z_ORDERS[s][::-1],
-                          (pl.ds(R // 2 * s, R // 2),), sems) for s in range(2)])
-        yield from steps(streams, 2)
+        for s in range(2):
+            for i in range(4):
+                for k, v in enumerate(unpack_from(m["xg", p, s][i // 2, i % 2], 2)):
+                    m["xf", p][i // 2, i % 2, pl.ds(16 * s, 16), pl.ds(128 * k, 128)] = (
+                        v.reshape(16, 128))
         if not have_b:
             b_copy.wait()
             have_b.append(p)
@@ -446,11 +516,11 @@
         yield from steps(streams, 4)
         ev = m["ev"][0, 0:1] + m["ev"][1, 0:1]
         eo = m["eo"][pl.ds(R * p + Q * col, Q), 0:1]
-        m["kc"][xmine + (p,)] = m["gw", p][xmine] / (ev - eo)
+        m["own"][p] = m["gw", p][xmine] / (ev - eo)
         mine = pl.ds(pl.multiple_of(256 * col, 128), 384)
         theirs = pl.ds(pl.multiple_of(256 - 256 * col, 128), 384)
-        m["kg"][rmine + (p, col)] = m["kc"][xmine + (p, slice(None), mine)]
-        m["win"][p] = m["kc"][xmine + (p, slice(None), theirs)]
+        m["kg"][rmine + (p, col)] = m["own"][p, :, mine]
+        m["win"][p] = m["own"][p, :, theirs]
         window = remote(m["win"].at[p], m["kg"].at[rmine + (p, col)], across)
         window.start()
         launch(7 + p, gather_piece(p))
@@ -462,6 +532,7 @@
         yield from steps(streams, 3)
 
     def gather_piece(p):
+        pack_into(m["kc"].at[xmine + (p,)], m["own"][p])
         yield from steps(start_all([
             gather_stream(place, m["kc"], XY, XY_ORDERS[p][::-1], (p,), sems)]), 4)
 
@@ -547,9 +618,12 @@
         for aux in range(8):
             if aux % 2 == 0:
                 yield
-            k0 = m["kc"][xy_bits(aux, 0)]
-            k1 = m["kc"][xy_bits(aux, 1)]
-            kh, kl = split(jnp.concatenate([k0[:, None], k1[:, None]], axis=1).reshape(128, 640))
+            rows = []
+            for p in range(PIECES):
+                for c in range(2):
+                    parts = unpack_from(m["kc"][xy_bits(aux, c) + (p,)], 2)
+                    rows.append(jnp.concatenate([v.reshape(Q, 128) for v in parts], axis=1))
+            kh, kl = split(jnp.concatenate(rows, axis=0))
             ch, cl = m["cvh"][:, pl.ds(640 * aux, 640)], m["cvl"][:, pl.ds(640 * aux, 640)]
             both = nt(ch, jnp.concatenate([kh, kl], axis=0))
             w = w + both[:, :128] + both[:, 128:] + nt(cl, kh)

time: 166 us -> 153 us (0.922)
  Pallas kernels: 162 us -> 150 us
    pallas_call x1, Pallas kernels: 162 us -> 150 us  [call(): pl.pallas_call(kernel, out_shape=outs, in_specs=in_specs, out_specs=jax.t...]
where the time goes in v4:
time: 153 us; the launch traced here: 152 us
  Pallas kernels  150 us (98%)
  local copies, waits for them, and re-layouts  2.86 us (2%)
    pallas_call x1, Pallas kernels, call(): pl.pallas_call(kernel, out_shape=outs, in_specs=in_specs, out_specs=jax.t...  150 us

profile of v4, /device:TPU:1, one launch (start us, length us, event | category | flops | bytes accessed | tf_op | source)
XLA Modules:
  0.0 152.5 jit_solution(7267570091356565915)
XLA Ops:
  0.0 1.2 broadcast_in_dim.6.ev_in
  1.2 149.6 %shard_map.64 = f32[384,128]{1,0:T(8,128)} custom-call(bf16[2,768,512]{2,1,0:T(8,128)(2,1)} %b_in.1, f32[768,384]{1,0:T(8,128)} %h_in.1, f32[768,1024]{1,0:T(8,128)} %c_in.1, f32[384,5120]{1,0:T(8,128)} %cv_in.1, f32[1,320]{1,0:T(1,128)} %broadcast_in_dim.6.ev_in, f32[1,128]{1,0:T(1,128)} %bitcast.1), custom_call_target="tpu_custom_call" | custom-call | tf_op jit(solution)/shard_map/pallas_call | solution.py:152
  150.9 1.6 %copy.8 = f32[384,128]{1,0:T(8,128)} copy(f32[384,128]{1,0:T(8,128)} %shard_map.64) | data formatting | bytes 393216

commit v5 on v4

--- a/solution.py
+++ b/solution.py
@@ -205,25 +205,31 @@
         peak = jnp.maximum(peak, jnp.max(jnp.abs(v), axis=0))
     peak = jnp.maximum(peak, 1e-30)
     n = [jnp.round(v * (LIMIT / peak)) for v in parts]
-    h3, h4 = jnp.floor(n[3] * (1 / 32)), jnp.floor(n[4] * (1 / 32))
-    words = [n[0] * 1024 + h3, n[1] * 1024 + h4,
-             n[2] * 1024 + ((n[3] - 32 * h3) * 32 + (n[4] - 32 * h4) - 512)]
-    if len(parts) == 8:
-        h = jnp.floor(n[7] * (1 / 128))
-        words += [n[5] * 256 + h, n[6] * 256 + (n[7] - 128 * h)]
+    words = []
+    if len(n) >= 5:
+        h3, h4 = jnp.floor(n[3] * (1 / 32)), jnp.floor(n[4] * (1 / 32))
+        words += [n[0] * 1024 + h3, n[1] * 1024 + h4,
+                  n[2] * 1024 + ((n[3] - 32 * h3) * 32 + (n[4] - 32 * h4) - 512)]
+        n = n[5:]
+    if n:
+        h = jnp.floor(n[2] * (1 / 128))
+        words += [n[0] * 256 + h, n[1] * 256 + (n[2] - 128 * h)]
     return peak * (1 / LIMIT), words
 
 
 def unpack(scale, words):
-    top = [jnp.floor((w + 512) * (1 / 1024)) for w in words[:3]]
-    h3, h4, rest = (w - 1024 * t for w, t in zip(words, top))
-    rest = rest + 512
-    l3 = jnp.floor(rest * (1 / 32))
-    n = top + [h3 * 32 + l3, h4 * 32 + (rest - 32 * l3)]
-    if len(words) == 5:
-        n5 = jnp.floor((words[3] + 128) * (1 / 256))
-        n6 = jnp.floor(words[4] * (1 / 256))
-        n += [n5, n6, (words[3] - 256 * n5) * 128 + (words[4] - 256 * n6)]
+    n = []
+    if len(words) >= 3:
+        n = [jnp.floor((w + 512) * (1 / 1024)) for w in words[:3]]
+        h3, h4, rest = (w - 1024 * t for w, t in zip(words, n))
+        rest = rest + 512
+        l3 = jnp.floor(rest * (1 / 32))
+        n += [h3 * 32 + l3, h4 * 32 + (rest - 32 * l3)]
+        words = words[3:]
+    if words:
+        n5 = jnp.floor((words[0] + 128) * (1 / 256))
+        n6 = jnp.floor(words[1] * (1 / 256))
+        n += [n5, n6, (words[0] - 256 * n5) * 128 + (words[1] - 256 * n6)]
     return [v * scale for v in n]
 
 
@@ -245,20 +251,13 @@
 PIECES = 4
 R = 128 // PIECES
 Q = R // 2
-G_CUTS = ((0, 16), (16, 8), (24, 8), (32, 8))
-G_ORDERS = [("za", "zb") + o[::-1] + ("cc",) for o in XY_ORDERS] + [XY_ORDERS[0] + ("za", "zb", "cc")]
 Z_ORDERS = (("za", "zb"), ("zb", "za"))
 SCHEDULE = [
-    0, 4, 1, 3, 4, 0, 2, 6, 6, 1, 6, 6, 3, 6, 0, 2, 1, 3, 0, 2, 1, 3, 0, 2,
-    1, 3, 0, 2, 1, 4, 3, 0, 2, 1, 3, 0, 4, 2, 1, 3, 0, 5, 2, 1, 3, 4, 2, 0,
-    1, 3, 2, 0, 5, 1, 3, 2, 0, 1, 3, 2, 0, 1, 3, 2, 0, 1, 5, 3, 2, 7, 8, 0,
-    5, 10, 1, 9, 3, 2, 7, 0, 8, 1, 10, 3, 9, 2, 0, 7, 1, 8, 0, 3, 10, 1, 2, 9,
-    3, 2, 12, 12, 12, 7, 8, 9, 12, 10, 11, 11, 11, 12, 11, 12, 11, 12, 12, 11, 12, 11, 12, 12,
+    0, 1, 2, 6, 6, 6, 0, 6, 6, 3, 1, 2, 0, 3, 1, 2, 0, 3, 4, 1, 2, 4, 0, 3,
+    4, 1, 2, 0, 3, 1, 4, 5, 2, 0, 4, 3, 1, 0, 2, 3, 1, 5, 0, 2, 3, 1, 0, 2,
+    3, 0, 1, 5, 7, 2, 3, 8, 5, 7, 1, 0, 9, 2, 0, 10, 3, 8, 9, 7, 1, 10, 1, 2,
+    8, 2, 9, 3, 3, 10, 12, 12, 7, 8, 9, 10, 11, 11, 11, 11, 12, 11, 11, 12, 11, 12,
 ]
-
-
-def grad_cuts(p):
-    return [((slice(None), pl.ds(128 * s, 128)), XY_ORDERS[s if s < 4 else p]) for s in range(5)]
 
 
 def scratch():
@@ -280,18 +279,20 @@
         bag.add(("xr", p), vm((4, R, 1024), F32))
         bag.add(("xw", p), vm((2, 2, R, 1024), F32))
         bag.add(("xf", p), vm((2, 2, R, 1024), F32))
-        bag.add(("yw", p), vm((2, 2, 2, 2, R, 384), F32))
+        bag.add(("yw", p), vm((4, 4, R, 384), F32))
         bag.add(("yb", p), vm((R, 384), F32))
-        bag.add(("gw", p), vm((2, 2, 2, 2, Q, 640), F32))
+        bag.add(("gw", p), vm((4, 4, Q, 640), F32))
         for s in range(2):
             for t, tiles in enumerate((4, 2)):
                 bag.add(("xout", p, s, t), vm((5 * tiles + 1, 8, 128), F32))
                 bag.add(("xin", p, s, t), vm((5 * tiles + 1, 8, 128), F32))
             bag.add(("xg", p, s), vm((2, 2, 11, 8, 128), F32))
-        for s in range(4):
-            bag.recvs(("yrec", p, s), 4, (R // 4, 384))
-        for s in range(5):
-            bag.recvs(("grec", p, s), 4, (Q, 128))
+        for s in range(2):
+            for name, rows, lanes, words in (("y", R // 2, 384, 2), ("g", Q // 2, 640, 3)):
+                packed = (3, words * rows // 2 + 1, 8, 128)
+                bag.add((name + "out", p, s), vm(packed, F32))
+                bag.add((name + "in", p, s), vm(packed, F32))
+                bag.add((name + "raw", p, s), vm((3, rows, lanes), F32))
     for s in range(2):
         bag.recvs(("hrec", s), 3, (64, 384))
     bag.add("hw", vm((2, 2, 2, 128, 384), F32))
@@ -299,10 +300,10 @@
     bag.add("own", vm((PIECES, Q, 640), F32))
     bag.add("kg", vm((2, 2, 2, PIECES, 2, Q, 384), F32))
     bag.add("win", vm((PIECES, Q, 384), F32))
-    bag.add("gs", vm((2, 2, 2, 2, 40, 128), F32))
-    for s, (_, n) in enumerate(G_CUTS):
-        bag.recvs(("gsrec", s), 4, (n, 128))
-    bag.add("gfull", vm((2,) * 7 + (40, 128), F32))
+    bag.add("gs", vm((2, 4, 80, 128), F32))
+    bag.add("gs1", vm((2, 3, 80, 128), F32))
+    bag.add("gs2", vm((2, 3, 80, 128), F32))
+    bag.add("gfull", vm((2, 4, 4, 2, 80, 128), F32))
     bag.add("wfull", vm((2, 2, 2, 384, 128), F32))
     bag.add("ghi", vm((1024, 1024), BF16))
     bag.add("glo", vm((1024, 1024), BF16))
@@ -326,6 +327,13 @@
     xmine = tuple(place.bit[d] for d in XY)
     rmine = tuple(place.bit[d] for d in ROW)
     zmine = rmine[:2]
+    at = {"x": 2 * col + place.aux % 2, "y": y, "z": z}
+    ring = {}
+    for d in (1, 2, 3):
+        xd, yd, zd = ((at[a] + d) % 4 for a in "xyz")
+        ring["x", d] = (2 * y + xd % 2, place.row, xd // 2)
+        ring["y", d] = (2 * yd + place.aux % 2, place.row, col)
+        ring["z", d] = (place.aux, 2 * zd + core, col)
 
     def remote(src, dst, device):
         s, r = sems.take()
@@ -352,9 +360,9 @@
         load_c(core, zz).start()
     barrier = pltpu.get_barrier_semaphore()
     dims = XY + ROW
-    for d in dims:
-        pl.semaphore_signal(barrier, inc=1, device_id=place.partner[d], device_id_type=MESH)
-    pl.semaphore_signal(barrier, inc=1, device_id=across, device_id_type=MESH)
+    greeted = [place.partner[d] for d in dims] + [across, ring["y", 2], ring["z", 2]]
+    for device in greeted:
+        pl.semaphore_signal(barrier, inc=1, device_id=device, device_id_type=MESH)
 
     @pl.when(y != z)
     def _():
@@ -381,11 +389,11 @@
 
     @pl.when(y != z)
     def _():
-        pl.semaphore_wait(barrier, len(dims) + 2)
+        pl.semaphore_wait(barrier, len(greeted) + 1)
 
     @pl.when(y == z)
     def _():
-        pl.semaphore_wait(barrier, len(dims) + 1)
+        pl.semaphore_wait(barrier, len(greeted))
 
     xc = [remote(m["xs", p], m["xr", p], place.partner["cc"]) for p in range(PIECES)]
     xc[0].start()
@@ -442,9 +450,52 @@
             yield
             copy.wait()
             for k, v in enumerate(unpack_from(m["xin", p, s, t][...], (4, 2)[t])):
-                at = mine + (pl.ds(128 * k, 128),)
-                work[at] = work[at] + v.reshape((2, 16, 128) if t == 0 else (16, 128))
+                spot = mine + (pl.ds(128 * k, 128),)
+                work[spot] = work[spot] + v.reshape((2, 16, 128) if t == 0 else (16, 128))
             done.append(d)
+
+    def two_rings(work, s, rows, out, wire, raw):
+        first, second = ("x", "y") if s == 0 else ("y", "x")
+        lanes = work.shape[-1]
+        tiles = (rows.size * 4) // 8
+
+        def index(i, j):
+            return ((i, j) if s == 0 else (j, i)) + (rows,)
+
+        copies = []
+        for d in (1, 2, 3):
+            pack_into(out.at[d - 1], work[index((at[first] + d) % 4, slice(None))])
+            copies.append(remote(out.at[d - 1], wire.at[d - 1], ring[first, d]))
+            copies[-1].start()
+        yield
+        mine = index(at[first], slice(None))
+        for c in copies:
+            c.wait()
+        got = [unpack_from(wire[d], tiles) for d in range(3)]
+        for k in range(lanes // 128):
+            place_k = mine + (pl.ds(128 * k, 128),)
+            v = (got[0][k] + got[1][k]) + got[2][k]
+            work[place_k] = work[place_k] + v.reshape(4, rows.size, 128)
+        copies = []
+        for d in (1, 2, 3):
+            copies.append(remote(work.at[index(at[first], (at[second] + d) % 4)],
+                                 raw.at[d - 1], ring[second, d]))
+            copies[-1].start()
+        yield
+        for c in copies:
+            c.wait()
+        mine = index(at[first], at[second])
+        work[mine] = (work[mine] + raw[0]) + (raw[1] + raw[2])
+
+    def ring_gather(full, index, axis):
+        copies = [remote(full.at[index], full.at[index], ring[axis, d]) for d in (1, 2, 3)]
+        for c in copies:
+            c.start()
+        return copies
+
+    def wait_all(copies):
+        for c in copies:
+            c.wait()
 
     def piece(p):
         yield
@@ -476,13 +527,12 @@
                 acc += nt(both[:, 512:], m["b"][side, 1, rows])
                 acc = acc[:4 * R] + acc[4 * R:]
                 for zz in range(4):
-                    m["yw", p][(xlo + half) % 2, half, (zz + zz // 2) % 2, zz // 2] = (
-                        acc[R * zz: R * zz + R])
+                    m["yw", p][2 * half + xlo, zz] = acc[R * zz: R * zz + R]
         streams = start_all([
-            scatter_stream(place, m["yw", p], XY, XY_ORDERS[s], (pl.ds(R // 4 * s, R // 4),),
-                           [m[("yrec", p, s), t] for t in range(4)], sems) for s in range(4)])
-        yield from steps(streams, 4)
-        swap = remote(m["yw", p].at[xmine], m["yb", p], swapped)
+            two_rings(m["yw", p], s, pl.ds(R // 2 * s, R // 2),
+                      m["yout", p, s], m["yin", p, s], m["yraw", p, s]) for s in range(2)])
+        yield from steps(streams, 2)
+        swap = remote(m["yw", p].at[at["x"], y], m["yb", p], swapped)
 
         @pl.when(y != z)
         def _():
@@ -490,7 +540,7 @@
 
         @pl.when(y == z)
         def _():
-            m["yb", p][...] = m["yw", p][xmine]
+            m["yb", p][...] = m["yw", p][at["x"], y]
 
         yield
         complete(4)
@@ -508,15 +558,14 @@
             acc = nn(both, m["cvh"][:, sl])
             acc = acc[:R] + acc[R:] + nn(hi, m["cvl"][:, sl])
             for c in range(2):
-                m["gw", p][xy_bits(aux, c)] = acc[Q * c: Q * c + Q]
+                m["gw", p][2 * c + aux % 2, aux // 2] = acc[Q * c: Q * c + Q]
         streams = start_all([
-            scatter_stream(place, m["gw", p], XY, order, tail,
-                           [m[("grec", p, s), t] for t in range(4)], sems)
-            for s, (tail, order) in enumerate(grad_cuts(p))])
-        yield from steps(streams, 4)
+            two_rings(m["gw", p], s, pl.ds(Q // 2 * s, Q // 2),
+                      m["gout", p, s], m["gin", p, s], m["graw", p, s]) for s in range(2)])
+        yield from steps(streams, 2)
         ev = m["ev"][0, 0:1] + m["ev"][1, 0:1]
         eo = m["eo"][pl.ds(R * p + Q * col, Q), 0:1]
-        m["own"][p] = m["gw", p][xmine] / (ev - eo)
+        m["own"][p] = m["gw", p][at["x"], y] / (ev - eo)
         mine = pl.ds(pl.multiple_of(256 * col, 128), 384)
         theirs = pl.ds(pl.multiple_of(256 - 256 * col, 128), 384)
         m["kg"][rmine + (p, col)] = m["own"][p, :, mine]
@@ -526,10 +575,14 @@
         launch(7 + p, gather_piece(p))
         yield
         window.wait()
-        streams = start_all([
-            gather_stream(place, m["kg"], ROW, Z_ORDERS[s] + ("cc",), (p, s), sems)
-            for s in range(2)])
-        yield from steps(streams, 3)
+        copies = ring_gather(m["kg"], rmine + (p,), "z")
+        yield
+        wait_all(copies)
+        block = m["kg"].at[:, :, core, p]
+        copy = remote(block, block, place.partner["cc"])
+        copy.start()
+        yield
+        copy.wait()
 
     def gather_piece(p):
         pack_into(m["kc"].at[xmine + (p,)], m["own"][p])
@@ -568,8 +621,8 @@
             for s in range(2):
                 order = Z_ORDERS[s] + ("cc",)
                 later = sum((differs[d] for d in order[k + 1:]), 0)
-                at = m["cg"].at[pl.ds(192 * s, 192)]
-                copy = remote(at, at, place.partner[order[k]])
+                half = m["cg"].at[pl.ds(192 * s, 192)]
+                copy = remote(half, half, place.partner[order[k]])
                 sends = later + differs[order[k]] == 0
                 takes = later + (1 - differs[order[k]]) == 0
                 copies.append((copy, sends, takes))
@@ -633,9 +686,7 @@
                           (pl.ds(192 * s, 192),), sems) for s in range(2)]), 3)
 
     def place_blocks(r):
-        chunks = [m["gfull"][(i // 8, (i // 4) % 2, (i // 2) % 2, i % 2) + row_bits(r)]
-                  for i in range(16)]
-        column = jnp.concatenate(chunks, axis=0)
+        column = m["gfull"][:, :, r // 2, r % 2].reshape(640, 128)
         for k in range(5):
             block = column[128 * k: 128 * k + 128]
             i = (r + k) % 8
@@ -657,16 +708,45 @@
             lh, ll = split(m["kg"][row_bits((place.row + k) % 8)].reshape(128, 384))
             accs.append(nt(lh, rh) + nt(lh, rl) + nt(ll, rh))
         acc = jnp.concatenate(accs, axis=0)
-        for k in range(16):
-            m["gs"][k // 8, (k // 4) % 2, (k // 2) % 2, k % 2] = acc[40 * k: 40 * k + 40]
-        yield from steps(start_all([
-            scatter_stream(place, m["gs"], XY, XY_ORDERS[s], (pl.ds(*cut),),
-                           [m[("gsrec", s), t] for t in range(4)], sems)
-            for s, cut in enumerate(G_CUTS)]), 4)
-        m["gfull"][xmine + rmine] = m["gs"][xmine]
-        yield from steps(start_all([
-            gather_stream(place, m["gfull"], XY + ROW, G_ORDERS[s], (pl.ds(8 * s, 8),), sems)
-            for s in range(5)]), 7)
+        m["gs"][...] = acc.reshape(2, 4, 80, 128)
+        firsts, seconds = ("x", "y"), ("y", "x")
+        copies = []
+        for s, axis in enumerate(firsts):
+            for d in (1, 2, 3):
+                copies.append(remote(m["gs"].at[s, (at[axis] + d) % 4], m["gs1"].at[s, d - 1],
+                                     ring[axis, d]))
+                copies[-1].start()
+        yield
+        wait_all(copies)
+        copies = []
+        for s, axis in enumerate(firsts):
+            mine = (s, at[axis])
+            m["gs"][mine] = ((m["gs"][mine] + m["gs1"][s, 0])
+                             + (m["gs1"][s, 1] + m["gs1"][s, 2]))
+            for d in (1, 2, 3):
+                copies.append(remote(m["gs"].at[mine], m["gs2"].at[s, d - 1],
+                                     ring[seconds[s], d]))
+                copies[-1].start()
+        yield
+        wait_all(copies)
+        copies = []
+        for s, axis in enumerate(firsts):
+            total = ((m["gs"][s, at[axis]] + m["gs2"][s, 0])
+                     + (m["gs2"][s, 1] + m["gs2"][s, 2]))
+            m["gfull"][s, at[axis], z, core] = total
+            copies += ring_gather(m["gfull"], (s, at[axis], z, core), "z")
+        yield
+        wait_all(copies)
+        copies = []
+        for s, axis in enumerate(firsts):
+            copies += ring_gather(m["gfull"], (s, at[axis], slice(None), core), axis)
+        yield
+        wait_all(copies)
+        block = m["gfull"].at[:, :, :, core]
+        copy = remote(block, block, place.partner["cc"])
+        copy.start()
+        yield
+        copy.wait()
 
     for p in range(PIECES):
         launch(p, piece(p))
@@ -697,12 +777,12 @@
     meansq = jnp.sum(total, axis=(0, 1), keepdims=True) / entries
     s1 = ROTATION_SCALE / jnp.sqrt(meansq + 1e-06)
     s2 = s1 * s1
-    at = pl.ds(pl.multiple_of(128 * place.row, 128), 128)
-    t[0, :, :128] = ghi[:, at]
-    t[0, :, 128:] = glo[:, at]
+    here = pl.ds(pl.multiple_of(128 * place.row, 128), 128)
+    t[0, :, :128] = ghi[:, here]
+    t[0, :, 128:] = glo[:, here]
     rows8 = lax.broadcasted_iota(jnp.int32, (1024, 128), 0)
     lanes8 = lax.broadcasted_iota(jnp.int32, (1024, 128), 1)
-    g1 = (ghi[:, at].astype(F32) + glo[:, at].astype(F32)) * s2
+    g1 = (ghi[:, here].astype(F32) + glo[:, here].astype(F32)) * s2
     eye = jnp.where(rows8 == lanes8 + 128 * place.row, 1.0, 0.0)
     acc_ref[0] = eye - g1 * 0.5
     acc_ref[1] = eye - g1 * (1.0 / 6.0)

time: 153 us -> 141 us (0.922)
  Pallas kernels: 150 us -> 138 us
    pallas_call x1, Pallas kernels: 150 us -> 138 us  [call(): pl.pallas_call(kernel, out_shape=outs, in_specs=in_specs, out_specs=jax.t...]
where the time goes in v5:
time: 141 us
  Pallas kernels  138 us (98%)
  local copies, waits for them, and re-layouts  2.86 us (2%)
    pallas_call x1, Pallas kernels, call(): pl.pallas_call(kernel, out_shape=outs, in_specs=in_specs, out_specs=jax.t...  138 us

profile of v5, /device:TPU:1, one launch (start us, length us, event | category | flops | bytes accessed | tf_op | source)
XLA Modules:
  0.0 140.7 jit_solution(10760879904709182783)
XLA Ops:
  0.0 1.2 broadcast_in_dim.6.ev_in
  1.2 137.8 %shard_map.64 = f32[384,128]{1,0:T(8,128)} custom-call(bf16[2,768,512]{2,1,0:T(8,128)(2,1)} %b_in.1, f32[768,384]{1,0:T(8,128)} %h_in.1, f32[768,1024]{1,0:T(8,128)} %c_in.1, f32[384,5120]{1,0:T(8,128)} %cv_in.1, f32[1,320]{1,0:T(1,128)} %broadcast_in_dim.6.ev_in, f32[1,128]{1,0:T(1,128)} %bitcast.1), custom_call_target="tpu_custom_call" | custom-call | tf_op jit(solution)/shard_map/pallas_call | solution.py:152
  139.1 1.6 %copy.8 = f32[384,128]{1,0:T(8,128)} copy(f32[384,128]{1,0:T(8,128)} %shard_map.64) | data formatting | bytes 393216

commit v6 on v5

--- a/solution.py
+++ b/solution.py
@@ -253,10 +253,10 @@
 Q = R // 2
 Z_ORDERS = (("za", "zb"), ("zb", "za"))
 SCHEDULE = [
-    0, 1, 2, 6, 6, 6, 0, 6, 6, 3, 1, 2, 0, 3, 1, 2, 0, 3, 4, 1, 2, 4, 0, 3,
-    4, 1, 2, 0, 3, 1, 4, 5, 2, 0, 4, 3, 1, 0, 2, 3, 1, 5, 0, 2, 3, 1, 0, 2,
-    3, 0, 1, 5, 7, 2, 3, 8, 5, 7, 1, 0, 9, 2, 0, 10, 3, 8, 9, 7, 1, 10, 1, 2,
-    8, 2, 9, 3, 3, 10, 12, 12, 7, 8, 9, 10, 11, 11, 11, 11, 12, 11, 11, 12, 11, 12,
+    0, 2, 1, 0, 3, 2, 1, 0, 3, 2, 4, 0, 1, 3, 4, 2, 0, 1, 3, 4, 2, 6, 1, 0,
+    3, 4, 5, 6, 6, 6, 6, 2, 1, 0, 4, 3, 2, 0, 1, 3, 5, 2, 1, 0, 3, 2, 1, 5,
+    0, 3, 5, 2, 0, 1, 3, 2, 1, 0, 0, 3, 7, 9, 8, 10, 2, 2, 1, 7, 9, 8, 10, 1,
+    3, 3, 9, 7, 8, 10, 12, 7, 9, 8, 10, 11, 11, 11, 12, 11, 12, 11, 11, 12, 11, 12,
 ]
 
 
@@ -303,7 +303,7 @@
     bag.add("gs", vm((2, 4, 80, 128), F32))
     bag.add("gs1", vm((2, 3, 80, 128), F32))
     bag.add("gs2", vm((2, 3, 80, 128), F32))
-    bag.add("gfull", vm((2, 4, 4, 2, 80, 128), F32))
+    bag.add("gfull", vm((2, 4, 4, 2, 7, 8, 128), F32))
     bag.add("wfull", vm((2, 2, 2, 384, 128), F32))
     bag.add("ghi", vm((1024, 1024), BF16))
     bag.add("glo", vm((1024, 1024), BF16))
@@ -643,7 +643,7 @@
 
     def cv_task():
         m["ev"][0] = jnp.zeros((8, 640), F32)
-        value = jnp.broadcast_to(ev_in[...], (8, 320))
+        value = jnp.broadcast_to(ev_in[...][None, :], (8, 320))
 
         @pl.when(col == 0)
         def _():
@@ -686,7 +686,9 @@
                           (pl.ds(192 * s, 192),), sems) for s in range(2)]), 3)
 
     def place_blocks(r):
-        column = m["gfull"][:, :, r // 2, r % 2].reshape(640, 128)
+        column = jnp.concatenate(
+            [v.reshape(16, 128) for s in range(2) for i in range(4)
+             for v in unpack_from(m["gfull"][s, i, r // 2, r % 2], 2)], axis=0)
         for k in range(5):
             block = column[128 * k: 128 * k + 128]
             i = (r + k) % 8
@@ -733,7 +735,11 @@
         for s, axis in enumerate(firsts):
             total = ((m["gs"][s, at[axis]] + m["gs2"][s, 0])
                      + (m["gs2"][s, 1] + m["gs2"][s, 2]))
-            m["gfull"][s, at[axis], z, core] = total
+            scale, words = pack([total[16 * i: 16 * i + 16].reshape(2, 8, 128) for i in range(5)])
+            mine = m["gfull"].at[s, at[axis], z, core]
+            mine[0] = scale
+            for i, w in enumerate(words):
+                mine[1 + 2 * i: 3 + 2 * i] = w
             copies += ring_gather(m["gfull"], (s, at[axis], z, core), "z")
         yield
         wait_all(copies)
@@ -819,7 +825,7 @@
     bag = scratch()
     return call(functools.partial(kernel, bag, entries), jax.ShapeDtypeStruct((384, 128), F32),
                 [ANY, ANY, ANY, ANY, VM, VM], bag.shapes, 0,
-                b_tensor, hcore, c_occ, c_virt, eps_virt[None, :], eps_occ[None, :])
+                b_tensor, hcore, c_occ, c_virt, eps_virt, eps_occ[None, :])
 
 
 def solution(mesh):

time: 141 us -> 136 us (0.965)
  Pallas kernels: 138 us -> 135 us
    pallas_call x1, Pallas kernels: 138 us -> 135 us  [call(): pl.pallas_call(kernel, out_shape=outs, in_specs=in_specs, out_specs=jax.t...]
where the time goes in v6:
time: 136 us
  Pallas kernels  135 us (99%)
  local copies, waits for them, and re-layouts  1.62 us (1%)
    pallas_call x1, Pallas kernels, call(): pl.pallas_call(kernel, out_shape=outs, in_specs=in_specs, out_specs=jax.t...  135 us

profile of v6, /device:TPU:1, one launch (start us, length us, event | category | flops | bytes accessed | tf_op | source)
XLA Modules:
  0.0 136.1 jit_solution(16520795287782259362)
XLA Ops:
  0.0 134.5 %shard_map.64 = f32[384,128]{1,0:T(8,128)} custom-call(bf16[2,768,512]{2,1,0:T(8,128)(2,1)} %b_in.1, f32[768,384]{1,0:T(8,128)} %h_in.1, f32[768,1024]{1,0:T(8,128)} %c_in.1, f32[384,5120]{1,0:T(8,128)} %cv_in.1, f32[320]{0:T(512)} %ev_in.1, f32[1,128]{1,0:T(1,128)} %bitcast.1), custom_call_target="tpu_custom_call" | custom-call | tf_op jit(solution)/shard_map/pallas_call | solution.py:152
  134.5 1.6 %copy.8 = f32[384,128]{1,0:T(8,128)} copy(f32[384,128]{1,0:T(8,128)} %shard_map.64) | data formatting | bytes 393216

commit v7 on v6

--- a/solution.py
+++ b/solution.py
@@ -253,10 +253,11 @@
 Q = R // 2
 Z_ORDERS = (("za", "zb"), ("zb", "za"))
 SCHEDULE = [
-    0, 2, 1, 0, 3, 2, 1, 0, 3, 2, 4, 0, 1, 3, 4, 2, 0, 1, 3, 4, 2, 6, 1, 0,
-    3, 4, 5, 6, 6, 6, 6, 2, 1, 0, 4, 3, 2, 0, 1, 3, 5, 2, 1, 0, 3, 2, 1, 5,
-    0, 3, 5, 2, 0, 1, 3, 2, 1, 0, 0, 3, 7, 9, 8, 10, 2, 2, 1, 7, 9, 8, 10, 1,
-    3, 3, 9, 7, 8, 10, 12, 7, 9, 8, 10, 11, 11, 11, 12, 11, 12, 11, 11, 12, 11, 12,
+    1, 0, 4, 4, 1, 2, 0, 3, 1, 2, 0, 3, 1, 2, 0, 3, 1, 2, 0, 3, 4, 2, 1, 3,
+    0, 4, 2, 5, 1, 6, 6, 6, 4, 6, 6, 3, 0, 1, 2, 3, 0, 5, 2, 1, 3, 0, 2, 1,
+    5, 3, 0, 1, 2, 5, 3, 0, 2, 1, 1, 3, 0, 0, 2, 2, 8, 9, 7, 10, 3, 3, 8, 9,
+    7, 10, 12, 8, 9, 7, 10, 12, 12, 9, 8, 7, 10, 11, 11, 11, 11, 11, 12, 12, 12, 11, 12, 12,
+    11,
 ]
 
 
@@ -411,7 +412,7 @@
             xc[p + 1].start()
     b_copy.start()
 
-    tasks, finished, have_b = {}, set(), []
+    tasks, finished, have_b, scales = {}, set(), [], []
 
     def advance(n):
         if n in tasks:
@@ -753,6 +754,45 @@
         copy.start()
         yield
         copy.wait()
+        ghi, glo, t, acc_ref = m["ghi"], m["glo"], m["t"], m["acc"]
+        r128 = lax.broadcasted_iota(jnp.int32, (128, 128), 0)
+        l128 = lax.broadcasted_iota(jnp.int32, (128, 128), 1)
+        total = jnp.zeros((128, 128), F32)
+        for r in range(8):
+            total = total + jnp.where(r128 == l128, place_blocks(r), 0.0)
+        meansq = jnp.sum(total, axis=(0, 1), keepdims=True) / entries
+        s1 = ROTATION_SCALE / jnp.sqrt(meansq + 1e-06)
+        s2 = s1 * s1
+        here = pl.ds(pl.multiple_of(128 * place.row, 128), 128)
+        t[0, :, :128] = ghi[:, here]
+        t[0, :, 128:] = glo[:, here]
+        rows8 = lax.broadcasted_iota(jnp.int32, (1024, 128), 0)
+        lanes8 = lax.broadcasted_iota(jnp.int32, (1024, 128), 1)
+        g1 = (ghi[:, here].astype(F32) + glo[:, here].astype(F32)) * s2
+        eye = jnp.where(rows8 == lanes8 + 128 * place.row, 1.0, 0.0)
+        acc_ref[0] = eye - g1 * 0.5
+        acc_ref[1] = eye - g1 * (1.0 / 6.0)
+        yield
+        coeff = [(1.0 / 24.0, 1.0 / 120.0), (-1.0 / 720.0, -1.0 / 5040.0), (1.0 / 40320.0, 0.0)]
+        for k, (ce, cs) in enumerate(coeff):
+            now, later = k % 2, (k + 1) % 2
+            scale = s2 * s2 if k == 0 else s2
+
+            @pl.loop(0, 4)
+            def _(i):
+                rs = pl.ds(pl.multiple_of(i * 256, 256), 256)
+                high = nn(ghi[rs], t[now])
+                power = (high[:, :128] + high[:, 128:] + nn(glo[rs], t[now, :, :128])) * scale
+                if k < 2:
+                    hi, lo = split(power)
+                    t[later, rs, :128] = hi
+                    t[later, rs, 128:] = lo
+                    acc_ref[1, rs] = acc_ref[1, rs] + power * cs
+                acc_ref[0, rs] = acc_ref[0, rs] + power * ce
+
+            if k < 2:
+                yield
+        scales.append(s1)
 
     for p in range(PIECES):
         launch(p, piece(p))
@@ -774,46 +814,12 @@
             advance(n)
         follow()
 
-    ghi, glo, t, acc_ref = m["ghi"], m["glo"], m["t"], m["acc"]
-    r128 = lax.broadcasted_iota(jnp.int32, (128, 128), 0)
-    l128 = lax.broadcasted_iota(jnp.int32, (128, 128), 1)
-    total = jnp.zeros((128, 128), F32)
-    for r in range(8):
-        total = total + jnp.where(r128 == l128, place_blocks(r), 0.0)
-    meansq = jnp.sum(total, axis=(0, 1), keepdims=True) / entries
-    s1 = ROTATION_SCALE / jnp.sqrt(meansq + 1e-06)
-    s2 = s1 * s1
-    here = pl.ds(pl.multiple_of(128 * place.row, 128), 128)
-    t[0, :, :128] = ghi[:, here]
-    t[0, :, 128:] = glo[:, here]
-    rows8 = lax.broadcasted_iota(jnp.int32, (1024, 128), 0)
-    lanes8 = lax.broadcasted_iota(jnp.int32, (1024, 128), 1)
-    g1 = (ghi[:, here].astype(F32) + glo[:, here].astype(F32)) * s2
-    eye = jnp.where(rows8 == lanes8 + 128 * place.row, 1.0, 0.0)
-    acc_ref[0] = eye - g1 * 0.5
-    acc_ref[1] = eye - g1 * (1.0 / 6.0)
-    coeff = [(1.0 / 24.0, 1.0 / 120.0), (-1.0 / 720.0, -1.0 / 5040.0), (1.0 / 40320.0, 0.0)]
-    for k, (ce, cs) in enumerate(coeff):
-        now, later = k % 2, (k + 1) % 2
-        scale = s2 * s2 if k == 0 else s2
-
-        @pl.loop(0, 4)
-        def _(i):
-            rs = pl.ds(pl.multiple_of(i * 256, 256), 256)
-            high = nn(ghi[rs], t[now])
-            power = (high[:, :128] + high[:, 128:] + nn(glo[rs], t[now, :, :128])) * scale
-            if k < 2:
-                hi, lo = split(power)
-                t[later, rs, :128] = hi
-                t[later, rs, 128:] = lo
-                acc_ref[1, rs] = acc_ref[1, rs] + power * cs
-            acc_ref[0, rs] = acc_ref[0, rs] + power * ce
-
+    acc_ref = m["acc"]
     e_hi, e_lo = split(acc_ref[0])
     c_hi, c_lo = split(m["cg"][...])
     both = nn(c_hi, jnp.concatenate([e_hi, e_lo], axis=1))
     result = both[:, :128] + both[:, 128:] + nn(c_lo, e_hi)
-    s_hi, s_lo = split(acc_ref[1] * s1)
+    s_hi, s_lo = split(acc_ref[1] * scales[0])
     w_all = jnp.concatenate([m["wfull"][row_bits(r)] for r in range(8)], axis=1)
     w_hi, w_lo = split(w_all)
     both = nn(w_hi, jnp.concatenate([s_hi, s_lo], axis=1))

time: 136 us -> 134 us (0.985)
  Pallas kernels: 135 us -> 132 us
    pallas_call x1, Pallas kernels: 135 us -> 132 us  [call(): pl.pallas_call(kernel, out_shape=outs, in_specs=in_specs, out_specs=jax.t...]
where the time goes in v7:
time: 134 us
  Pallas kernels  132 us (99%)
  local copies, waits for them, and re-layouts  1.62 us (1%)
    pallas_call x1, Pallas kernels, call(): pl.pallas_call(kernel, out_shape=outs, in_specs=in_specs, out_specs=jax.t...  132 us

profile of v7, /device:TPU:1, one launch (start us, length us, event | category | flops | bytes accessed | tf_op | source)
XLA Modules:
  0.0 133.6 jit_solution(4324349221699355733)
XLA Ops:
  0.0 132.0 %shard_map.64 = f32[384,128]{1,0:T(8,128)} custom-call(bf16[2,768,512]{2,1,0:T(8,128)(2,1)} %b_in.1, f32[768,384]{1,0:T(8,128)} %h_in.1, f32[768,1024]{1,0:T(8,128)} %c_in.1, f32[384,5120]{1,0:T(8,128)} %cv_in.1, f32[320]{0:T(512)} %ev_in.1, f32[1,128]{1,0:T(1,128)} %bitcast.1), custom_call_target="tpu_custom_call" | custom-call | tf_op jit(solution)/shard_map/pallas_call | solution.py:152
  132.0 1.6 %copy.8 = f32[384,128]{1,0:T(8,128)} copy(f32[384,128]{1,0:T(8,128)} %shard_map.64) | data formatting | bytes 393216
